TPU v7x, 32 devices: a whole 2x2x4 slice. The times are simulated.
32 devices in a mesh: dom: 4 (over y, x), sub: 8 (over z, core).
Axes of the slice: x: 2, y: 2, z: 4, core: 2. Of those that a mesh axis runs over, the one named last changes fastest.
Arguments:
- coords: float32 [3, 8192], P(None, ('dom', 'sub')), may hold values from -6 to 6
- direction: float32 [3, 8192], P(None, ('dom', 'sub')), may hold values from -6 to 6
- connect: int32 [4, 32768], P(None, ('dom', 'sub')), may hold values from 0 to 383
- shape_inv: float32 [9, 32768], P(None, ('dom', 'sub')), may hold values from -3.5 to 3.5
- weight: float32 [32768], P(('dom', 'sub')), may hold values from 0.3 to 9
- send_node: int32 [32, 128], P(('dom', 'sub')), may hold values from 0 to 255
- recv_slot: int32 [32, 128], P(('dom', 'sub')), may hold values from 0 to 127, each once within a row
Outputs:
- gradient: float32 [4, 3, 8192], P(None, None, ('dom', 'sub'))
- energy: float32 [4], replicated
- min_det: float32 [4], replicated
Inputs may be any that keep to these rules, and one draw needn't show every extreme that they name: `connect`: each tetrahedron's corners are local node numbers: owned nodes below 256, ghost slots above. `send_node`: owned node numbers; a node may be listed several times. `recv_slot`: each row is a permutation of the ghost slots.
All inputs are finite; a program needn't handle non-finite values.
Results may differ from a plain program's by a relative error of at most 0.0001.
Values sent between devices are 32-bit elements; how exact they have to be, the bound alone decides.
No kernel may reach another device: no remote copies, remote signals or barrier semaphores. Data moves between devices by JAX's collectives and lax.ppermute only.
A program may use at most 64 MiB of HBM per device.

v0:
```python
import jax
import jax.numpy as jnp
from jax import lax
from jax.sharding import PartitionSpec as P

TRIALS = 4


step_scales = (1.0, 0.5, 0.25, 0.125)


def passed_along(shard, axis, by):
    count = lax.axis_size(axis)
    return lax.ppermute(shard, axis, [(i, (i + by) % count) for i in range(count)])


def jacobian(places, connect, shape_inv):
    elem_count = connect.shape[1]
    corners_all = jnp.take(places, connect.reshape(-1), axis=1).reshape(3, 4, elem_count)
    differ = corners_all[:, 1:] - corners_all[:, :1]
    return [
        [
            differ[row_index, 0] * shape_inv[col_index]
            + differ[row_index, 1] * shape_inv[3 + col_index]
            + differ[row_index, 2] * shape_inv[6 + col_index]
            for col_index in range(3)
        ]
        for row_index in range(3)
    ]


def cofactor(matrix):
    return [
        [
            matrix[1][1] * matrix[2][2] - matrix[1][2] * matrix[2][1],
            matrix[1][2] * matrix[2][0] - matrix[1][0] * matrix[2][2],
            matrix[1][0] * matrix[2][1] - matrix[1][1] * matrix[2][0],
        ],
        [
            matrix[0][2] * matrix[2][1] - matrix[0][1] * matrix[2][2],
            matrix[0][0] * matrix[2][2] - matrix[0][2] * matrix[2][0],
            matrix[0][1] * matrix[2][0] - matrix[0][0] * matrix[2][1],
        ],
        [
            matrix[0][1] * matrix[1][2] - matrix[0][2] * matrix[1][1],
            matrix[0][2] * matrix[1][0] - matrix[0][0] * matrix[1][2],
            matrix[0][0] * matrix[1][1] - matrix[0][1] * matrix[1][0],
        ],
    ]


def element_dets(places, connect, shape_inv):
    matrix = jacobian(places, connect, shape_inv)
    cofac = cofactor(matrix)
    return matrix[0][0] * cofac[0][0] + matrix[0][1] * cofac[0][1] + matrix[0][2] * cofac[0][2]


def barrier_shift(lowest):
    return lowest - 1.0 - jnp.abs(lowest)


def element_grad(places, connect, shape_inv, weight, shift, node_count):
    matrix = jacobian(places, connect, shape_inv)
    cofac = cofactor(matrix)
    determ = matrix[0][0] * cofac[0][0] + matrix[0][1] * cofac[0][1] + matrix[0][2] * cofac[0][2]
    lifted = determ - shift
    squares = matrix[0][0] * matrix[0][0]
    for row_index in range(3):
        for col_index in range(3):
            if row_index + col_index > 0:
                squares = squares + matrix[row_index][col_index] * matrix[row_index][col_index]
    power = lifted ** (-2.0 / 3.0)
    energy_part = jnp.sum(weight * squares * power) / 3.0
    scale_jac = weight * power * (2.0 / 3.0)
    scale_cof = weight * squares * power / lifted * (2.0 / 9.0)
    djac = [
        [
            scale_jac * matrix[row_index][col_index] - scale_cof * cofac[row_index][col_index]
            for col_index in range(3)
        ]
        for row_index in range(3)
    ]
    flat_index = connect.reshape(-1)
    rows_out = []
    for row_index in range(3):
        dedge = [
            djac[row_index][0] * shape_inv[3 * edge_index]
            + djac[row_index][1] * shape_inv[3 * edge_index + 1]
            + djac[row_index][2] * shape_inv[3 * edge_index + 2]
            for edge_index in range(3)
        ]
        rows_out.append(
            jnp.concatenate([-(dedge[0] + dedge[1] + dedge[2]), dedge[0], dedge[1], dedge[2]])
        )
    combined = jnp.stack(rows_out)
    targets = flat_index[None, :] + node_count * jnp.arange(3, dtype=jnp.int32)[:, None]
    summed = jax.ops.segment_sum(
        combined.reshape(-1), targets.reshape(-1), num_segments=3 * node_count
    )
    return (energy_part, summed.reshape(3, node_count))


def global_min(values):
    inner_min = lax.pmin(values, "sub")
    return lax.pmin(inner_min, "dom")


def global_sum(values):
    inner_sum = lax.psum(values, "sub")
    return lax.psum(inner_sum, "dom")


def send_back(ghost_grads, sends, slots, node_count):
    share_len = sends.shape[0] // 4
    ordered = ghost_grads[..., slots]
    leading = ordered.shape[:-1]
    blocks_all = ordered.reshape(leading + (4, share_len))
    came_all = []
    for block_index, offset in ((0, -1), (1, 1)):
        came_all.append(passed_along(blocks_all[..., block_index, :], "dom", offset))
    for block_index, offset in ((2, -1), (3, 1)):
        came_all.append(passed_along(blocks_all[..., block_index, :], "sub", offset))
    joined = jnp.concatenate(came_all, axis=-1)
    return jnp.zeros(leading + (node_count,), jnp.float32).at[..., sends].add(joined)


def per_device(coords, direction, connect, shape_inv, weight, send_node, recv_slot):
    node_count = coords.shape[1]
    sends = send_node[0]
    slots = recv_slot[0]
    share_len = sends.shape[0] // 4
    both = jnp.concatenate([coords, direction], axis=0)
    outgoing = jnp.take(both, sends, axis=1).reshape(6, 4, share_len)
    arrived = []
    for block_index, offset in ((0, 1), (1, -1)):
        arrived.append(passed_along(outgoing[:, block_index], "dom", offset))
    for block_index, offset in ((2, 1), (3, -1)):
        arrived.append(passed_along(outgoing[:, block_index], "sub", offset))
    arrived_rows = jnp.concatenate(arrived, axis=1)
    ghosts = jnp.zeros_like(arrived_rows).at[:, slots].set(arrived_rows)
    local = jnp.concatenate([both, ghosts], axis=1)
    local_count = local.shape[1]
    local_coords = local[:3]
    local_dir = local[3:]
    elem_total = connect.shape[1] * lax.axis_size("dom") * lax.axis_size("sub")
    lows = []
    totals = []
    grads = []
    for trial_index in range(TRIALS):
        places = local_coords + step_scales[trial_index] * local_dir
        lowest = global_min(jnp.min(element_dets(places, connect, shape_inv)))
        energy_part, grad_rows = element_grad(
            places, connect, shape_inv, weight, barrier_shift(lowest), local_count
        )
        totals.append(global_sum(energy_part))
        owned = grad_rows[:, :node_count] + send_back(
            grad_rows[:, node_count:], sends, slots, node_count
        )
        lows.append(lowest)
        grads.append(owned)
    lowest_all = jnp.stack(lows)
    energy = jnp.stack(totals) / elem_total
    gradient = jnp.stack(grads)
    return (gradient, energy, lowest_all)


def solution(mesh):
    placed = (
        P(None, ("dom", "sub")),
        P(None, ("dom", "sub")),
        P(None, ("dom", "sub")),
        P(None, ("dom", "sub")),
        P(("dom", "sub")),
        P(("dom", "sub"), None),
        P(("dom", "sub"), None),
    )
    return jax.shard_map(
        per_device,
        mesh=mesh,
        in_specs=placed,
        out_specs=(P(None, None, ("dom", "sub")), P(), P()),
        check_vma=False,
    )
```

profile of v0, /device:TPU:0, one launch (start us, length us, event | category | flops | bytes accessed | tf_op | source)
XLA Modules:
  0.0 508.8 jit_solution(15034063371528856785)
XLA Ops:
  3.4 1.3 reduce.3
  4.8 3.0 collective-permute-start
  7.8 1.0 collective-permute-start.1
  8.9 3.5 collective-permute-start.3
  12.4 0.7 fusion.3
  13.1 0.7 compare_and_fusion
  13.9 0.7 copy.196
  15.2 1.1 fusion.26
  16.7 0.9 scatter_custom_fusion
  17.9 10.8 %gather_fusion.6 = f32[4096,3]{1,0:T(8,128)S(1)} fusion(f32[3,384]{0,1:T(8,128)S(1)} %get-tuple-element.136, s32[4096]{0:T(1024)S(1)} %fusion.3), kind=kCustom, calls=%fused_computation.1.clone | custom fusion | bytes 114688 | tf_op jit(solution)/shard_map/jit(_take)/gather | solution.py:19
  28.6 14.1 %gather_fusion.7 = f32[4096,3]{1,0:T(8,128)} fusion(f32[3,384]{0,1:T(8,128)S(1)} %get-tuple-element.137, s32[4096]{0:T(1024)S(1)} %fusion.3), kind=kCustom, calls=%fused_computation.2.clone | custom fusion | bytes 114688 | tf_op jit(solution)/shard_map/jit(_take)/gather | solution.py:19
  42.7 14.1 %gather_fusion.8 = f32[4096,3]{1,0:T(8,128)} fusion(f32[3,384]{0,1:T(8,128)S(1)} %get-tuple-element.138, s32[4096]{0:T(1024)S(1)} %fusion.3), kind=kCustom, calls=%fused_computation.3.clone | custom fusion | bytes 114688 | tf_op jit(solution)/shard_map/jit(_take)/gather | solution.py:19
  56.8 14.1 %gather_fusion.5 = f32[4096,3]{1,0:T(8,128)} fusion(f32[3,384]{0,1:T(8,128)S(1)} %get-tuple-element.95, s32[4096]{0:T(1024)S(1)} %fusion.3), kind=kCustom, calls=%fused_computation.clone | custom fusion | bytes 114688 | tf_op jit(solution)/shard_map/jit(_take)/gather | solution.py:19
  70.9 4.5 broadcast_select_fusion.3
  75.4 1.2 slice.273
  76.6 0.9 slice_bitcast_fusion.3
  77.5 1.3 slice.290
  78.7 0.8 slice_bitcast_fusion.2
  79.7 0.8 slice_bitcast_fusion.1
  80.6 0.8 slice_bitcast_fusion
  81.5 2.0 copy.162
  83.5 1.2 copy.123
  84.8 2.0 copy.169
  86.8 1.2 copy.132
  88.8 1.3 copy.141
  93.6 15.0 %all-reduce.1 = (f32[]{:T(128)}, f32[]{:T(128)}, f32[]{:T(128)}, f32[]{:T(128)}) all-reduce(f32[]{:T(128)} %get-tuple-element.123, f32[]{:T(128)} %get-tuple-element.110, f32[]{:T(128)} %get-tuple-element.97, f32[]{:T(128)} %get-tuple-element.82), channel_id=1, replica_groups=mesh['dom'=4,'sub'=8] {'sub'}, use_global_device_ids=true, to_apply=%region_17.19 | all-reduce | flops 4 | bytes 32 | tf_op jit(solution)/shard_map/pmin | solution.py:104
  108.6 10.1 %all-reduce.3 = (f32[]{:T(128)}, f32[]{:T(128)}, f32[]{:T(128)}, f32[]{:T(128)}) all-reduce(f32[]{:T(128)} %get-tuple-element.14, f32[]{:T(128)} %get-tuple-element.15, f32[]{:T(128)} %get-tuple-element.16, f32[]{:T(128)} %get-tuple-element.17), channel_id=1, replica_groups=mesh['dom'=4,'sub'=8] {'dom'}, use_global_device_ids=true, to_apply=%region_18.20 | all-reduce | flops 4 | bytes 32 | tf_op jit(solution)/shard_map/pmin | solution.py:105
  126.2 78.9 %scatter_custom_fusion.1 = f32[1152]{0:T(1024)S(1)} fusion(s32[12288]{0:T(1024)S(1)} %reshape.266, f32[12288]{0:T(1024)S(1)} %reshape.268, f32[]{:T(128)} %constant.19.clone.1), kind=kCustom, calls=%fused_computation.224 | custom fusion | flops 12288 | bytes 4612 | tf_op jit(solution)/shard_map/scatter-add | solution.py:97
  205.2 78.9 %scatter_custom_fusion.3 = f32[1152]{0:T(1024)S(1)} fusion(s32[12288]{0:T(1024)S(1)} %reshape.266, f32[12288]{0:T(1024)S(1)} %reshape.284, f32[]{:T(128)} %constant.19.clone.1), kind=kCustom, calls=%fused_computation.222 | custom fusion | flops 12288 | bytes 4612 | tf_op jit(solution)/shard_map/scatter-add | solution.py:97
  284.2 78.9 %scatter_custom_fusion.5 = f32[1152]{0:T(1024)S(1)} fusion(s32[12288]{0:T(1024)S(1)} %reshape.266, f32[12288]{0:T(1024)S(1)} %reshape.300, f32[]{:T(128)} %constant.19.clone.1), kind=kCustom, calls=%fused_computation.220 | custom fusion | flops 12288 | bytes 4612 | tf_op jit(solution)/shard_map/scatter-add | solution.py:97
  364.0 78.9 %scatter_custom_fusion.7 = f32[1152]{0:T(1024)S(1)} fusion(s32[12288]{0:T(1024)S(1)} %reshape.266, f32[12288]{0:T(1024)S(1)} %reshape.316, f32[]{:T(128)} %constant.19.clone.1), kind=kCustom, calls=%fused_computation.218 | custom fusion | flops 12288 | bytes 4612 | tf_op jit(solution)/shard_map/scatter-add | solution.py:97
  446.2 2.5 collective-permute-start.4
  450.6 3.1 collective-permute-start.10
  456.1 3.1 pad_maximum_fusion.19
  459.3 14.2 %all-reduce = (f32[]{:T(128)}, f32[]{:T(128)}, f32[]{:T(128)}, f32[]{:T(128)}) all-reduce(f32[]{:T(128)S(6)} %div.34, f32[]{:T(128)S(6)} %div.33, f32[]{:T(128)S(6)} %div.32, f32[]{:T(128)S(6)} %div.31), channel_id=1, replica_groups=mesh['dom'=4,'sub'=8] {'sub'}, use_global_device_ids=true, to_apply=%region_31.33 | all-reduce | flops 4 | bytes 32 | tf_op jit(solution)/shard_map/psum | solution.py:109
  473.5 10.9 %all-reduce.2 = (f32[1]{0:T(128)}, f32[1]{0:T(128)}, f32[1]{0:T(128)}, f32[1]{0:T(128)}) all-reduce(f32[1]{0:T(128)} %bitcast.119, f32[1]{0:T(128)} %bitcast.118, f32[1]{0:T(128)} %bitcast.117, f32[1]{0:T(128)} %bitcast.116), channel_id=1, replica_groups=mesh['dom'=4,'sub'=8] {'dom'}, use_global_device_ids=true, to_apply=%region_32.34 | all-reduce | flops 4 | bytes 32 | tf_op jit(solution)/shard_map/psum | solution.py:110
  484.3 3.1 maximum_multiply_fusion
  488.0 2.0 collective-permute-start.9
  490.0 1.0 collective-permute-start.12
  491.1 1.1 collective-permute-start.13
  492.7 1.8 collective-permute-start.14
  494.5 2.2 collective-permute-start.16
  496.9 1.3 scatter_fusion
  498.5 3.3 collective-permute-start.18
  501.8 1.3 scatter_fusion.1
  503.3 1.3 scatter_fusion.2
  504.8 1.8 collective-permute-done.19
  506.7 1.3 scatter_fusion.3
  (154 shorter events, 20.0 us)
Async XLA Ops:
  4.8 11.6 %collective-permute-start = (f32[6,32]{1,0:T(8,128)S(1)}, f32[6,32]{1,0:T(8,128)S(1)}, u32[]{:S(2)}, u32[]{:S(2)}) collective-permute-start(f32[6,32]{1,0:T(8,128)S(1)} %get-tuple-element.268), channel_id=1, source_target_pairs={{0,8},{8,16},{16,24},{24,0},{1,9},{9,17},{17,25},{25,1},{2,10},{10... | collective-permute-start | bytes 2312 | tf_op jit(solution)/shard_map/ppermute | solution.py:14
  7.8 8.6 %collective-permute-start.1 = (f32[6,32]{1,0:T(8,128)S(1)}, f32[6,32]{1,0:T(8,128)S(1)}, u32[]{:S(2)}, u32[]{:S(2)}) collective-permute-start(f32[6,32]{1,0:T(8,128)S(1)} %get-tuple-element.271), channel_id=1, source_target_pairs={{0,24},{8,0},{16,8},{24,16},{1,25},{9,1},{17,9},{25,17},{2,26},{10... | collective-permute-start | bytes 2312 | tf_op jit(solution)/shard_map/ppermute | solution.py:14
  8.9 7.6 %collective-permute-start.2 = (f32[6,32]{1,0:T(8,128)S(1)}, f32[6,32]{1,0:T(8,128)S(1)}, u32[]{:S(2)}, u32[]{:S(2)}) collective-permute-start(f32[6,32]{1,0:T(8,128)S(1)} %get-tuple-element.270), channel_id=1, source_target_pairs={{0,1},{1,2},{2,3},{3,4},{4,5},{5,6},{6,7},{7,0},{8,9},{9,10},{10,1... | collective-permute-start | bytes 2312 | tf_op jit(solution)/shard_map/ppermute | solution.py:14
  8.9 7.6 %collective-permute-start.3 = (f32[6,32]{1,0:T(8,128)S(1)}, f32[6,32]{1,0:T(8,128)S(1)}, u32[]{:S(2)}, u32[]{:S(2)}) collective-permute-start(f32[6,32]{1,0:T(8,128)S(1)} %get-tuple-element.269), channel_id=1, source_target_pairs={{0,7},{1,0},{2,1},{3,2},{4,3},{5,4},{6,5},{7,6},{8,15},{9,8},{10,9... | collective-permute-start | bytes 2312 | tf_op jit(solution)/shard_map/ppermute | solution.py:14
  88.7 2.0 copy-start
  88.8 35.0 %copy-start.1 = (f32[1024]{0:T(1024)S(1)}, f32[1024]{0:T(1024)}, u32[]{:S(2)}) copy-start(f32[1024]{0:T(1024)} %param.13) | copy-start | bytes 12292
  446.2 41.6 %collective-permute-start.4 = (f32[3,32]{1,0:T(4,128)S(1)}, f32[3,32]{1,0:T(4,128)S(1)}, u32[]{:S(2)}, u32[]{:S(2)}) collective-permute-start(f32[3,32]{1,0:T(4,128)S(1)} %bitcast.309), channel_id=1, source_target_pairs={{0,24},{8,0},{16,8},{24,16},{1,25},{9,1},{17,9},{25,17},{2,26},{10... | collective-permute-start | bytes 1160 | tf_op jit(solution)/shard_map/ppermute | solution.py:14
  448.8 39.1 %collective-permute-start.5 = (f32[3,32]{1,0:T(4,128)S(1)}, f32[3,32]{1,0:T(4,128)S(1)}, u32[]{:S(2)}, u32[]{:S(2)}) collective-permute-start(f32[3,32]{1,0:T(4,128)S(1)} %bitcast.307), channel_id=1, source_target_pairs={{0,8},{8,16},{16,24},{24,0},{1,9},{9,17},{17,25},{25,1},{2,10},{10... | collective-permute-start | bytes 1160 | tf_op jit(solution)/shard_map/ppermute | solution.py:14
  448.9 39.1 %collective-permute-start.6 = (f32[3,32]{1,0:T(4,128)S(1)}, f32[3,32]{1,0:T(4,128)S(1)}, u32[]{:S(2)}, u32[]{:S(2)}) collective-permute-start(f32[3,32]{1,0:T(4,128)S(1)} %bitcast.306), channel_id=1, source_target_pairs={{0,7},{1,0},{2,1},{3,2},{4,3},{5,4},{6,5},{7,6},{8,15},{9,8},{10,9... | collective-permute-start | bytes 1160 | tf_op jit(solution)/shard_map/ppermute | solution.py:14
  449.1 40.9 %collective-permute-start.7 = (f32[3,32]{1,0:T(4,128)S(1)}, f32[3,32]{1,0:T(4,128)S(1)}, u32[]{:S(2)}, u32[]{:S(2)}) collective-permute-start(f32[3,32]{1,0:T(4,128)S(1)} %bitcast.305), channel_id=1, source_target_pairs={{0,1},{1,2},{2,3},{3,4},{4,5},{5,6},{6,7},{7,0},{8,9},{9,10},{10,1... | collective-permute-start | bytes 1160 | tf_op jit(solution)/shard_map/ppermute | solution.py:14
  450.6 40.4 %collective-permute-start.10 = (f32[3,32]{1,0:T(4,128)S(1)}, f32[3,32]{1,0:T(4,128)S(1)}, u32[]{:S(2)}, u32[]{:S(2)}) collective-permute-start(f32[3,32]{1,0:T(4,128)S(1)} %bitcast.310), channel_id=1, source_target_pairs={{0,7},{1,0},{2,1},{3,2},{4,3},{5,4},{6,5},{7,6},{8,15},{9,8},{10,9... | collective-permute-start | bytes 1160 | tf_op jit(solution)/shard_map/ppermute | solution.py:14
  487.8 4.9 collective-permute-start.11
  487.9 6.6 %collective-permute-start.8 = (f32[3,32]{1,0:T(4,128)S(1)}, f32[3,32]{1,0:T(4,128)S(1)}, u32[]{:S(2)}, u32[]{:S(2)}) collective-permute-start(f32[3,32]{1,0:T(4,128)S(1)} %bitcast.304), channel_id=1, source_target_pairs={{0,24},{8,0},{16,8},{24,16},{1,25},{9,1},{17,9},{25,17},{2,26},{10... | collective-permute-start | bytes 1160 | tf_op jit(solution)/shard_map/ppermute | solution.py:14
  488.0 6.5 %collective-permute-start.9 = (f32[3,32]{1,0:T(4,128)S(1)}, f32[3,32]{1,0:T(4,128)S(1)}, u32[]{:S(2)}, u32[]{:S(2)}) collective-permute-start(f32[3,32]{1,0:T(4,128)S(1)} %bitcast.303), channel_id=1, source_target_pairs={{0,8},{8,16},{16,24},{24,0},{1,9},{9,17},{17,25},{25,1},{2,10},{10... | collective-permute-start | bytes 1160 | tf_op jit(solution)/shard_map/ppermute | solution.py:14
  490.0 8.4 %collective-permute-start.12 = (f32[3,32]{1,0:T(4,128)S(1)}, f32[3,32]{1,0:T(4,128)S(1)}, u32[]{:S(2)}, u32[]{:S(2)}) collective-permute-start(f32[3,32]{1,0:T(4,128)S(1)} %bitcast.299), channel_id=1, source_target_pairs={{0,24},{8,0},{16,8},{24,16},{1,25},{9,1},{17,9},{25,17},{2,26},{10... | collective-permute-start | bytes 1160 | tf_op jit(solution)/shard_map/ppermute | solution.py:14
  491.1 7.4 %collective-permute-start.13 = (f32[3,32]{1,0:T(4,128)S(1)}, f32[3,32]{1,0:T(4,128)S(1)}, u32[]{:S(2)}, u32[]{:S(2)}) collective-permute-start(f32[3,32]{1,0:T(4,128)S(1)} %bitcast.298), channel_id=1, source_target_pairs={{0,8},{8,16},{16,24},{24,0},{1,9},{9,17},{17,25},{25,1},{2,10},{10... | collective-permute-start | bytes 1160 | tf_op jit(solution)/shard_map/ppermute | solution.py:14
  492.7 9.0 %collective-permute-start.14 = (f32[3,32]{1,0:T(4,128)S(1)}, f32[3,32]{1,0:T(4,128)S(1)}, u32[]{:S(2)}, u32[]{:S(2)}) collective-permute-start(f32[3,32]{1,0:T(4,128)S(1)} %bitcast.297), channel_id=1, source_target_pairs={{0,7},{1,0},{2,1},{3,2},{4,3},{5,4},{6,5},{7,6},{8,15},{9,8},{10,9... | collective-permute-start | bytes 1160 | tf_op jit(solution)/shard_map/ppermute | solution.py:14
  494.5 7.3 %collective-permute-start.15 = (f32[3,32]{1,0:T(4,128)S(1)}, f32[3,32]{1,0:T(4,128)S(1)}, u32[]{:S(2)}, u32[]{:S(2)}) collective-permute-start(f32[3,32]{1,0:T(4,128)S(1)} %bitcast.296), channel_id=1, source_target_pairs={{0,1},{1,2},{2,3},{3,4},{4,5},{5,6},{6,7},{7,0},{8,9},{9,10},{10,1... | collective-permute-start | bytes 1160 | tf_op jit(solution)/shard_map/ppermute | solution.py:14
  494.5 10.2 %collective-permute-start.16 = (f32[3,32]{1,0:T(4,128)S(1)}, f32[3,32]{1,0:T(4,128)S(1)}, u32[]{:S(2)}, u32[]{:S(2)}) collective-permute-start(f32[3,32]{1,0:T(4,128)S(1)} %bitcast.295), channel_id=1, source_target_pairs={{0,24},{8,0},{16,8},{24,16},{1,25},{9,1},{17,9},{25,17},{2,26},{10... | collective-permute-start | bytes 1160 | tf_op jit(solution)/shard_map/ppermute | solution.py:14
  498.4 6.3 %collective-permute-start.17 = (f32[3,32]{1,0:T(4,128)S(1)}, f32[3,32]{1,0:T(4,128)S(1)}, u32[]{:S(2)}, u32[]{:S(2)}) collective-permute-start(f32[3,32]{1,0:T(4,128)S(1)} %bitcast.302), channel_id=1, source_target_pairs={{0,8},{8,16},{16,24},{24,0},{1,9},{9,17},{17,25},{25,1},{2,10},{10... | collective-permute-start | bytes 1160 | tf_op jit(solution)/shard_map/ppermute | solution.py:14
  498.5 6.3 %collective-permute-start.18 = (f32[3,32]{1,0:T(4,128)S(1)}, f32[3,32]{1,0:T(4,128)S(1)}, u32[]{:S(2)}, u32[]{:S(2)}) collective-permute-start(f32[3,32]{1,0:T(4,128)S(1)} %bitcast.301), channel_id=1, source_target_pairs={{0,7},{1,0},{2,1},{3,2},{4,3},{5,4},{6,5},{7,6},{8,15},{9,8},{10,9... | collective-permute-start | bytes 1160 | tf_op jit(solution)/shard_map/ppermute | solution.py:14
  501.7 4.8 collective-permute-start.19
where the time goes:
time: 509 us
  other arithmetic  343 us (67%)
  local copies, waits for them, and re-layouts  78.6 us (15%)
  blocking collectives  50.1 us (10%)
  starting transfers between devices  25.2 us (5%)
  between operations  8.97 us (2%)
    scatter-add x4, other arithmetic, element_grad(): jax.ops.segment_sum(combined.reshape(-1), targets.reshape(-1), num_segmen...  315 us
    gather x4, local copies, waits for them, and re-layouts, jacobian(): jnp.take(places, connect.reshape(-1), axis=1).reshape(3, 4, elem_count)  53 us
    ppermute x20, starting transfers between devices, passed_along(): lax.ppermute(shard, axis, [(i, (i + by) % count) for i in range(count)])  25.2 us
    pmin x1, blocking collectives, global_min(): inner_min = lax.pmin(values, 'sub')  15 us
    psum x1, blocking collectives, global_sum(): inner_sum = lax.psum(values, 'sub')  14.2 us
    psum x1, blocking collectives, global_sum(): return lax.psum(inner_sum, 'dom')  10.9 us
  transfers between devices with their start and end apart: 20, of which 2 were waited for; matrix products, arithmetic and copies ran while one was open for 4% of the time, Pallas kernels for 0%

commit v1 on v0

v1 whole, which is shorter than its diff:
```python
import functools

import jax
import jax.numpy as jnp
from jax import lax
from jax.experimental import pallas as pl
from jax.experimental.pallas import tpu as pltpu
from jax.sharding import PartitionSpec as P

TRIALS = 4
AXES = ("dom", "sub")
LANES = 128
SUBS = 8


def lane_ids():
    return lax.broadcasted_iota(jnp.int32, (SUBS, LANES), 1)


def sub_ids():
    return lax.broadcasted_iota(jnp.int32, (SUBS, LANES), 0)


def spread(row):
    return jnp.broadcast_to(row, (SUBS, LANES))


def picked(table, index):
    return jnp.take_along_axis(table, index, axis=1, mode="promise_in_bounds")


def step_lengths():
    trial = sub_ids() & (TRIALS - 1)
    return jnp.where(
        trial == 0, 1.0, jnp.where(trial == 1, 0.5, jnp.where(trial == 2, 0.25, 0.125))
    ).astype(jnp.float32)


def halves(ref, row, block, blocks):
    first = spread(ref[row : row + 1, block * LANES : (block + 1) * LANES])
    later = blocks + block
    second = spread(ref[row : row + 1, later * LANES : (later + 1) * LANES])
    return jnp.where(sub_ids() < TRIALS, first, second)


def split_three(value):
    high = value.astype(jnp.bfloat16)
    rest = value - high.astype(jnp.float32)
    mid = rest.astype(jnp.bfloat16)
    low = (rest - mid.astype(jnp.float32)).astype(jnp.bfloat16)
    return [high, mid, low]


def marks(row, count):
    places = lax.broadcasted_iota(jnp.int32, (count, row.shape[1]), 0)
    hit = places == jnp.broadcast_to(row, (count, row.shape[1]))
    return jnp.where(hit, 1.0, 0.0).astype(jnp.bfloat16)


def by_marks(left, right):
    return lax.dot_general(
        left, right, (((1,), (1,)), ((), ())), preferred_element_type=jnp.float32
    )


def send_kernel(coords, direction, send, out, table):
    table[...] = jnp.zeros_like(table)
    table[0:3, :] = coords[...]
    table[3:6, :] = direction[...]
    index = spread(send[...])
    low = index & (LANES - 1)
    first = picked(table[:, :LANES], low)
    second = picked(table[:, LANES:], low)
    out[...] = jnp.where(index < LANES, first, second)


def cofactor(m):
    return [
        [
            m[1][1] * m[2][2] - m[1][2] * m[2][1],
            m[1][2] * m[2][0] - m[1][0] * m[2][2],
            m[1][0] * m[2][1] - m[1][1] * m[2][0],
        ],
        [
            m[0][2] * m[2][1] - m[0][1] * m[2][2],
            m[0][0] * m[2][2] - m[0][2] * m[2][0],
            m[0][1] * m[2][0] - m[0][0] * m[2][1],
        ],
        [
            m[0][1] * m[1][2] - m[0][2] * m[1][1],
            m[0][2] * m[1][0] - m[0][0] * m[1][2],
            m[0][0] * m[1][1] - m[0][1] * m[1][0],
        ],
    ]


def det_kernel(
    blocks, coords, direction, got0, got1, got2, got3, connect, inverse, slots,
    low_out, jac_out, table,
):
    lane = lane_ids()
    group = lane // 32
    order = marks(slots[...], LANES)
    entry = lax.broadcasted_iota(jnp.int32, (16, LANES), 1).astype(jnp.bfloat16)
    came_at = by_marks(entry, order)[:SUBS].astype(jnp.int32)
    arrived = jnp.where(
        group == 0,
        got0[...],
        jnp.where(group == 1, got1[...], jnp.where(group == 2, got2[...], got3[...])),
    )
    ghosts = picked(arrived, came_at)
    owned = coords.shape[1]
    table[0:3, :owned] = coords[...]
    table[3:6, :owned] = direction[...]
    table[:, owned:] = ghosts
    steps = step_lengths()
    tiles = table.shape[1] // LANES
    places = [
        [
            spread(table[comp : comp + 1, tile * LANES : (tile + 1) * LANES])
            + steps * spread(table[3 + comp : 4 + comp, tile * LANES : (tile + 1) * LANES])
            for tile in range(tiles)
        ]
        for comp in range(3)
    ]
    lowest = None
    for block in range(blocks):
        corners = []
        for corner in range(4):
            index = halves(connect, corner, block, blocks)
            low = index & (LANES - 1)
            in_first = index < LANES
            in_second = index < 2 * LANES
            corners.append(
                [
                    jnp.where(
                        in_first,
                        picked(places[comp][0], low),
                        jnp.where(
                            in_second,
                            picked(places[comp][1], low),
                            picked(places[comp][2], low),
                        ),
                    )
                    for comp in range(3)
                ]
            )
        weights = [halves(inverse, row, block, blocks) for row in range(9)]
        jac = []
        for comp in range(3):
            edges = [corners[k][comp] - corners[0][comp] for k in (1, 2, 3)]
            jac.append(
                [
                    edges[0] * weights[col]
                    + edges[1] * weights[3 + col]
                    + edges[2] * weights[6 + col]
                    for col in range(3)
                ]
            )
        cofac = cofactor(jac)
        det = jac[0][0] * cofac[0][0] + jac[0][1] * cofac[0][1] + jac[0][2] * cofac[0][2]
        lowest = det if lowest is None else jnp.minimum(lowest, det)
        for comp in range(3):
            for col in range(3):
                jac_out[3 * comp + col, :, block * LANES : (block + 1) * LANES] = jac[comp][col]
    least = spread_lanes(jnp.min(lowest, axis=1, keepdims=True))
    at_trial = jnp.where(lane == (sub_ids() & (TRIALS - 1)), least, jnp.inf)
    row = jnp.min(at_trial, axis=0, keepdims=True)
    low_out[...] = jnp.broadcast_to(row, low_out.shape)


def spread_lanes(column):
    return jnp.broadcast_to(column, (SUBS, LANES))


def grad_kernel(
    blocks, sub_count, dom_count, lows, jac_in, weight, connect, inverse, slots,
    own_out, back_out, low_out,
):
    lane, sub = lane_ids(), sub_ids()
    lowest_row = jnp.min(lows[...], axis=0, keepdims=True)
    low_out[...] = lowest_row
    mine = jnp.where(lane == (sub & (TRIALS - 1)), spread(lowest_row), 0.0)
    lowest = spread_lanes(jnp.sum(mine, axis=1, keepdims=True))
    shift = lowest - 1.0 - jnp.abs(lowest)
    energy = None
    terms = [[[] for _ in range(3)] for _ in range(4)]
    for block in range(blocks):
        cut = slice(block * LANES, (block + 1) * LANES)
        jac = [[jac_in[3 * comp + col, :, cut] for col in range(3)] for comp in range(3)]
        cofac = cofactor(jac)
        det = jac[0][0] * cofac[0][0] + jac[0][1] * cofac[0][1] + jac[0][2] * cofac[0][2]
        squares = jac[0][0] * jac[0][0]
        for comp in range(3):
            for col in range(3):
                if comp + col > 0:
                    squares = squares + jac[comp][col] * jac[comp][col]
        lifted = det - shift
        power = jnp.exp(jnp.log(lifted) * (-2.0 / 3.0))
        heavy = jnp.where(
            sub < TRIALS,
            spread(weight[block : block + 1, :]),
            spread(weight[blocks + block : blocks + block + 1, :]),
        )
        scaled = heavy * power
        part = scaled * squares
        energy = part if energy is None else energy + part
        scale_jac = scaled * (2.0 / 3.0)
        scale_cof = part / lifted * (2.0 / 9.0)
        weights = [halves(inverse, row, block, blocks) for row in range(9)]
        for comp in range(3):
            djac = [scale_jac * jac[comp][col] - scale_cof * cofac[comp][col] for col in range(3)]
            edges = [
                djac[0] * weights[3 * k] + djac[1] * weights[3 * k + 1] + djac[2] * weights[3 * k + 2]
                for k in range(3)
            ]
            terms[0][comp].append(-(edges[0] + edges[1] + edges[2]))
            for k in range(3):
                terms[k + 1][comp].append(edges[k])
    width = blocks * LANES
    local = own_out.shape[1] + LANES
    sums = [None, None]
    for corner in range(4):
        values = jnp.concatenate(
            [jnp.concatenate(terms[corner][comp], axis=1) for comp in range(3)], axis=0
        )
        left = jnp.concatenate(split_three(values), axis=0)
        for half in range(2):
            row = connect[corner : corner + 1, half * width : (half + 1) * width]
            found = by_marks(left, marks(row, local))
            sums[half] = found if sums[half] is None else sums[half] + found
    rows = 3 * SUBS
    sums = [s[:rows] + s[rows : 2 * rows] + s[2 * rows :] for s in sums]
    upper = lax.broadcasted_iota(jnp.int32, (SUBS, local), 0) < TRIALS
    ghosts = []
    for comp in range(3):
        cut = slice(comp * SUBS, (comp + 1) * SUBS)
        mixed = jnp.where(upper, sums[0][cut], sums[1][cut])
        both = mixed + pltpu.roll(mixed, TRIALS, 0)
        own_out[cut, :] = both[:, : local - LANES]
        ghosts.append(picked(both[:, local - LANES :], spread(slots[...])))
    energy = spread_lanes(jnp.sum(energy, axis=1, keepdims=True))
    energy = energy + pltpu.roll(energy, TRIALS, 0)
    back_out[...] = jnp.broadcast_to(energy[None, :TRIALS], back_out.shape)
    dom, part = lax.axis_index("dom"), lax.axis_index("sub")
    targets = (
        lax.rem(dom + dom_count - 1, dom_count) * sub_count + part,
        lax.rem(dom + 1, dom_count) * sub_count + part,
        dom * sub_count + lax.rem(part + sub_count - 1, sub_count),
        dom * sub_count + lax.rem(part + 1, sub_count),
    )
    group = lane // 32
    for k in range(4):
        tile = energy
        for comp in range(3):
            turned = (32 * (comp - k)) % LANES
            moved = pltpu.roll(ghosts[comp], turned, 1) if turned else ghosts[comp]
            tile = jnp.where(group == comp, moved, tile)
        back_out[targets[k]] = tile[:TRIALS]


def final_kernel(
    sub_count, dom_count, elem_total, back, own, send, low, gradient, energy_out, low_out
):
    lane = lane_ids()[:TRIALS]
    sub = sub_ids()[:TRIALS]
    group = lane // 32
    dom, part = lax.axis_index("dom"), lax.axis_index("sub")
    sources = (
        lax.rem(dom + 1, dom_count) * sub_count + part,
        lax.rem(dom + dom_count - 1, dom_count) * sub_count + part,
        dom * sub_count + lax.rem(part + 1, sub_count),
        dom * sub_count + lax.rem(part + sub_count - 1, sub_count),
    )
    came = [back[sources[k]] for k in range(4)]
    came = [jnp.concatenate([tile, tile], axis=0) for tile in came]
    wide = lane_ids() // 32
    rows = []
    for comp in range(3):
        whole = None
        for k in range(4):
            turned = (32 * (k - comp)) % LANES
            moved = pltpu.roll(came[k], turned, 1) if turned else came[k]
            whole = moved if whole is None else jnp.where(wide == k, moved, whole)
        rows.append(whole)
    left = jnp.concatenate(split_three(jnp.concatenate(rows, axis=0)), axis=0)
    found = by_marks(left, marks(send[...], own.shape[1]))
    height = 3 * SUBS
    found = found[:height] + found[height : 2 * height] + found[2 * height :]
    found = found + own[...]
    for comp in range(3):
        gradient[:, comp, :] = found[comp * SUBS : comp * SUBS + TRIALS]
    total = jnp.sum(back[...], axis=0)
    total = jnp.broadcast_to(total[:, LANES - 1 :], (TRIALS, LANES))
    total = jnp.sum(jnp.where(lane == sub, total, 0.0), axis=0, keepdims=True)
    energy_out[...] = total[:, :TRIALS] / 3.0 / elem_total
    low_out[...] = low[:, :TRIALS]


def exchanged(tile, axis, sent_by):
    count = lax.axis_size(axis)
    return lax.ppermute(tile, axis, [(i, (i + sent_by) % count) for i in range(count)])


def per_device(coords, direction, connect, shape_inv, weight, send_node, recv_slot):
    doms, subs = lax.axis_size("dom"), lax.axis_size("sub")
    count = doms * subs
    owned = coords.shape[1]
    elems = connect.shape[1]
    blocks = elems // (2 * LANES)
    local = owned + recv_slot.shape[1]
    f32 = jnp.float32
    vmem = pltpu.CompilerParams(vmem_limit_bytes=32 * 1024 * 1024)
    outgoing = pl.pallas_call(
        send_kernel,
        out_shape=jax.ShapeDtypeStruct((SUBS, LANES), f32),
        scratch_shapes=[pltpu.VMEM((SUBS, owned), f32)],
        compiler_params=vmem,
        name="outgoing_nodes",
    )(coords, direction, send_node)
    came = (
        exchanged(outgoing, "dom", 1),
        exchanged(outgoing, "dom", -1),
        exchanged(outgoing, "sub", 1),
        exchanged(outgoing, "sub", -1),
    )
    lows, jac = pl.pallas_call(
        functools.partial(det_kernel, blocks),
        out_shape=(
            jax.ShapeDtypeStruct((count, LANES), f32),
            jax.ShapeDtypeStruct((9, SUBS, elems // 2), f32),
        ),
        scratch_shapes=[pltpu.VMEM((SUBS, local), f32)],
        compiler_params=vmem,
        name="jacobian_dets",
    )(coords, direction, *came, connect, shape_inv, recv_slot)
    lows = lax.all_to_all(lows.reshape(count, 1, LANES), AXES, 0, 0).reshape(count, LANES)
    own, back, low = pl.pallas_call(
        functools.partial(grad_kernel, blocks, subs, doms),
        out_shape=(
            jax.ShapeDtypeStruct((3 * SUBS, owned), f32),
            jax.ShapeDtypeStruct((count, TRIALS, LANES), f32),
            jax.ShapeDtypeStruct((1, LANES), f32),
        ),
        compiler_params=vmem,
        name="element_gradients",
    )(lows, jac, weight.reshape(elems // LANES, LANES), connect, shape_inv, recv_slot)
    back = lax.all_to_all(back, AXES, 0, 0)
    gradient, energy, lowest = pl.pallas_call(
        functools.partial(final_kernel, subs, doms, float(elems * count)),
        out_shape=(
            jax.ShapeDtypeStruct((TRIALS, 3, owned), f32),
            jax.ShapeDtypeStruct((1, TRIALS), f32),
            jax.ShapeDtypeStruct((1, TRIALS), f32),
        ),
        compiler_params=vmem,
        name="owner_sums",
    )(back, own, send_node, low)
    return gradient, energy.reshape(TRIALS), lowest.reshape(TRIALS)


def solution(mesh):
    placed = (
        P(None, AXES),
        P(None, AXES),
        P(None, AXES),
        P(None, AXES),
        P(AXES),
        P(AXES, None),
        P(AXES, None),
    )
    return jax.shard_map(
        per_device,
        mesh=mesh,
        in_specs=placed,
        out_specs=(P(None, None, AXES), P(), P()),
        check_vma=False,
    )
```

time: 509 us -> 39 us (0.08)
  other arithmetic: 343 us -> 0 us
  local copies, waits for them, and re-layouts: 78.6 us -> 5.53 us
  blocking collectives: 50.1 us -> 18.5 us
  starting transfers between devices: 25.2 us -> 6.94 us
  between operations: 8.97 us -> 0.66 us
    scatter-add x8 -> x0, other arithmetic: 321 us -> none  [the longest x4 315 us: element_grad(): jax.ops.segment_sum(combined.reshape(-1), targets.reshape(-1), num_segmen...]
    gather x10 -> x0, local copies, waits for them, and re-layouts: 56.4 us -> none  [the longest x4 53 us: jacobian(): jnp.take(places, connect.reshape(-1), axis=1).reshape(3, 4, elem_count)]
    pmin x2 -> x0, blocking collectives: 25.1 us -> none  [the longest x1 15 us: global_min(): inner_min = lax.pmin(values, 'sub')]
    psum x2 -> x0, blocking collectives: 25.1 us -> none  [the longest x1 14.2 us: global_sum(): inner_sum = lax.psum(values, 'sub')]
    all_to_all x0 -> x2, blocking collectives: none -> 18.5 us  [the longest x1 9.42 us: per_device(): lax.all_to_all(lows.reshape(count, 1, LANES), AXES, 0, 0)]
    ppermute x20 -> x4, starting transfers between devices: 25.2 us -> 6.94 us  [exchanged(): lax.ppermute(tile, axis, [(i, (i + sent_by) % count) for i in range(count)])]
    sub x8 -> x0, local copies, waits for them, and re-layouts: 7.31 us -> none  [jacobian(): differ = corners_all[:, 1:] - corners_all[:, :1]]
    select_n x4 -> x0, other arithmetic: 5.82 us -> none  [the longest x1 4.5 us: jacobian(): jnp.take(places, connect.reshape(-1), axis=1).reshape(3, 4, elem_count)]
  transfers between devices with their start and end apart: 20 -> 4, of which waited for: 2 -> 2; matrix products, arithmetic and copies ran while one was open for 4% -> 0% of each run, Pallas kernels for 0% -> 0%
where the time goes in v1:
time: 39 us; the launch traced here: 38.6 us
  blocking collectives  18.5 us (47%)
  starting transfers between devices  6.94 us (18%)
  local copies, waits for them, and re-layouts  5.53 us (14%)
  waiting for transfers between devices  4.5 us (12%)
  Pallas kernels  2.49 us (6%)
  between operations  0.66 us (2%)
    all_to_all x1, blocking collectives, per_device(): lax.all_to_all(lows.reshape(count, 1, LANES), AXES, 0, 0)  9.42 us
    all_to_all x1, blocking collectives, per_device(): back = lax.all_to_all(back, AXES, 0, 0)  9.08 us
    ppermute x4, starting transfers between devices, exchanged(): lax.ppermute(tile, axis, [(i, (i + sent_by) % count) for i in range(count)])  6.94 us
    unnamed x21, local copies, waits for them, and re-layouts  5.53 us
    ppermute x4, waiting for transfers between devices, exchanged(): lax.ppermute(tile, axis, [(i, (i + sent_by) % count) for i in range(count)])  4.5 us
    pallas_call x1, Pallas kernels, per_device(): pl.pallas_call(functools.partial(grad_kernel, blocks, subs, doms), out_sh...  1.27 us
  transfers between devices with their start and end apart: 4, of which 2 were waited for; matrix products, arithmetic and copies ran while one was open for 0% of the time, Pallas kernels for 0%

profile of v1, /device:TPU:0, one launch (start us, length us, event | category | flops | bytes accessed | tf_op | source)
XLA Modules:
  0.0 38.6 jit_solution(14955781390425958835)
XLA Ops:
  0.6 0.0 copy-start.4
  0.6 0.7 %copy-done.4 = f32[3,256]{1,0:T(4,128)S(1)} copy-done((f32[3,256]{1,0:T(4,128)S(1)}, f32[3,256]{1,0:T(4,128)}, u32[]{:S(2)}) %copy-start.4) | copy-done | bytes 3096
  1.3 0.0 copy-start.5
  1.3 0.7 %copy-done.5 = f32[3,256]{1,0:T(4,128)S(1)} copy-done((f32[3,256]{1,0:T(4,128)S(1)}, f32[3,256]{1,0:T(4,128)}, u32[]{:S(2)}) %copy-start.5) | copy-done | bytes 3096
  2.0 0.0 copy-start.8
  2.0 0.7 %copy-done.8 = s32[1,128]{1,0:T(1,128)S(1)} copy-done((s32[1,128]{1,0:T(1,128)S(1)}, s32[1,128]{1,0:T(1,128)}, u32[]{:S(2)}) %copy-start.8) | copy-done | bytes 536
  2.7 0.0 copy-start.7
  2.7 0.1 outgoing_nodes.1
  2.7 4.5 %collective-permute-start.3 = (f32[8,128]{1,0:T(8,128)S(1)}, f32[8,128]{1,0:T(8,128)S(1)}, u32[]{:S(2)}, u32[]{:S(2)}) collective-permute-start(f32[8,128]{1,0:T(8,128)S(1)} %outgoing_nodes.1), channel_id=1, source_target_pairs={{0,7},{1,0},{2,1},{3,2},{4,3},{5,4},{6,5},{7,6},{8,15},{9,8},{10,9... | collective-permute-start | bytes 12296 | tf_op jit(solution)/shard_map/ppermute | solution.py:302
  7.2 0.0 collective-permute-start.2
  7.2 2.4 %collective-permute-start.1 = (f32[8,128]{1,0:T(8,128)S(1)}, f32[8,128]{1,0:T(8,128)S(1)}, u32[]{:S(2)}, u32[]{:S(2)}) collective-permute-start(f32[8,128]{1,0:T(8,128)S(1)} %outgoing_nodes.1), channel_id=1, source_target_pairs={{0,24},{8,0},{16,8},{24,16},{1,25},{9,1},{17,9},{25,17},{2,26},{10... | collective-permute-start | bytes 12296 | tf_op jit(solution)/shard_map/ppermute | solution.py:302
  9.7 0.0 collective-permute-start
  9.7 0.0 collective-permute-done.3.got3
  9.7 2.4 %collective-permute-done.2.got2 = f32[8,128]{1,0:T(8,128)S(1)} collective-permute-done((f32[8,128]{1,0:T(8,128)S(1)}, f32[8,128]{1,0:T(8,128)S(1)}, u32[]{:S(2)}, u32[]{:S(2)}) %collective-permute-start.2) | collective-permute-done | bytes 4128 | tf_op jit(solution)/shard_map/ppermute | solution.py:302
  12.1 0.0 collective-permute-done.1.got1
  12.1 2.1 %collective-permute-done.got0 = f32[8,128]{1,0:T(8,128)S(1)} collective-permute-done((f32[8,128]{1,0:T(8,128)S(1)}, f32[8,128]{1,0:T(8,128)S(1)}, u32[]{:S(2)}, u32[]{:S(2)}) %collective-permute-start) | collective-permute-done | bytes 4128 | tf_op jit(solution)/shard_map/ppermute | solution.py:302
  14.2 0.0 copy-done.7
  14.2 0.0 copy-start
  14.2 0.8 %copy-done = f32[9,1024]{1,0:T(8,128)S(1)} copy-done((f32[9,1024]{1,0:T(8,128)S(1)}, f32[9,1024]{1,0:T(8,128)}, u32[]{:S(2)}) %copy-start) | copy-done | bytes 36888
  15.0 0.0 copy-start.2
  15.0 0.7 %copy-done.2 = s32[4,1024]{1,0:T(4,128)S(1)} copy-done((s32[4,1024]{1,0:T(4,128)S(1)}, s32[4,1024]{1,0:T(4,128)}, u32[]{:S(2)}) %copy-start.2) | copy-done | bytes 16408
  15.8 0.0 copy-start.1
  15.8 0.5 %jacobian_dets.1 = (f32[32,128]{1,0:T(8,128)S(1)}, f32[9,8,512]{2,1,0:T(8,128)S(1)}) custom-call(f32[3,256]{1,0:T(4,128)S(1)} %copy-done.4, f32[3,256]{1,0:T(4,128)S(1)} %copy-done.5, f32[8,128]{1,0:T(8,128)S(1)} %collective-permute-done.got0, f32[8,128]{1,0:T(8,128)S(1)} %collective-permute-done.1.got1, f32[8,128]{1,0:T(8,128)S(1)} %collective-permute-done.2.got2, ...), custom_call_target="tpu_custom_call" | custom-call | tf_op jit(solution)/shard_map/jacobian_dets/pallas_call | solution.py:327
  16.2 0.0 copy-start.3
  16.2 9.4 %all_to_all.10 = f32[32,1,128]{2,1,0:T(1,128)S(1)} all-to-all(f32[32,1,128]{2,1,0:T(1,128)S(1)} %bitcast.8), channel_id=1, replica_groups=mesh['dom'=4,'sub'=8] {'dom','sub'}, dimensions={0} | all-to-all | bytes 32768 | tf_op jit(solution)/shard_map/all_to_all | solution.py:337
  25.7 0.0 copy-start.6
  25.7 0.0 copy-done.1
  25.7 0.0 copy-done.3
  25.7 0.7 %copy-done.6 = f32[1024]{0:T(1024)S(1)} copy-done((f32[1024]{0:T(1024)S(1)}, f32[1024]{0:T(1024)}, u32[]{:S(2)}) %copy-start.6) | copy-done | bytes 4120
  26.4 1.3 %element_gradients.1 = (f32[24,256]{1,0:T(8,128)S(1)}, f32[32,4,128]{2,1,0:T(4,128)S(1)}, f32[1,128]{1,0:T(1,128)S(1)}) custom-call(f32[32,128]{1,0:T(8,128)S(1)} %bitcast.7, f32[9,8,512]{2,1,0:T(8,128)S(1)} %get-tuple-element.12.jac_in, f32[8,128]{1,0:T(8,128)S(1)} %bitcast.9, s32[4,1024]{1,0:T(4,128)S(1)} %copy-done.3, f32[9,1024]{1,0:T(8,128)S(1)} %copy-done.1, ...), custom_call_target="tpu_custom_call" | custom-call | tf_op jit(solution)/shard_map/element_gradients/pallas_call | solution.py:338
  27.6 9.1 %all_to_all.11.back = f32[32,4,128]{2,1,0:T(4,128)S(1)} all-to-all(f32[32,4,128]{2,1,0:T(4,128)S(1)} %get-tuple-element.13), channel_id=1, replica_groups=mesh['dom'=4,'sub'=8] {'dom','sub'}, dimensions={0} | all-to-all | bytes 131072 | tf_op jit(solution)/shard_map/all_to_all | solution.py:348
  36.7 0.0 copy-start.9
  36.7 0.7 %copy-done.9 = s32[1,128]{1,0:T(1,128)S(1)} copy-done((s32[1,128]{1,0:T(1,128)S(1)}, s32[1,128]{1,0:T(1,128)}, u32[]{:S(2)}) %copy-start.9) | copy-done | bytes 536
  37.4 0.7 %owner_sums.1 = (f32[4,3,256]{2,1,0:T(4,128)S(1)}, f32[1,4]{1,0:T(1,128)}, f32[1,4]{1,0:T(1,128)}) custom-call(f32[32,4,128]{2,1,0:T(4,128)S(1)} %all_to_all.11.back, f32[24,256]{1,0:T(8,128)S(1)} %get-tuple-element.14.own, s32[1,128]{1,0:T(1,128)S(1)} %copy-done.9, f32[1,128]{1,0:T(1,128)S(1)} %get-tuple-element.15.low), custom_call_target="tpu_custom_call" | custom-call | tf_op jit(solution)/shard_map/owner_sums/pallas_call | solution.py:349
  38.0 0.6 %copy.12 = f32[4,3,256]{2,0,1:T(4,128)} copy(f32[4,3,256]{2,1,0:T(4,128)S(1)} %get-tuple-element.22) | data formatting | bytes 24576
Async XLA Ops:
  0.6 0.7 %copy-start.4 = (f32[3,256]{1,0:T(4,128)S(1)}, f32[3,256]{1,0:T(4,128)}, u32[]{:S(2)}) copy-start(f32[3,256]{1,0:T(4,128)} %coords.3) | copy-start | bytes 9220
  1.3 0.7 %copy-start.5 = (f32[3,256]{1,0:T(4,128)S(1)}, f32[3,256]{1,0:T(4,128)}, u32[]{:S(2)}) copy-start(f32[3,256]{1,0:T(4,128)} %direction.3) | copy-start | bytes 9220
  2.0 0.7 %copy-start.8 = (s32[1,128]{1,0:T(1,128)S(1)}, s32[1,128]{1,0:T(1,128)}, u32[]{:S(2)}) copy-start(s32[1,128]{1,0:T(1,128)} %send.3) | copy-start | bytes 1540
  2.7 11.5 %copy-start.7 = (s32[1,128]{1,0:T(1,128)S(1)}, s32[1,128]{1,0:T(1,128)}, u32[]{:S(2)}) copy-start(s32[1,128]{1,0:T(1,128)} %slots.3) | copy-start | bytes 1540
  2.7 6.9 %collective-permute-start.3 = (f32[8,128]{1,0:T(8,128)S(1)}, f32[8,128]{1,0:T(8,128)S(1)}, u32[]{:S(2)}, u32[]{:S(2)}) collective-permute-start(f32[8,128]{1,0:T(8,128)S(1)} %outgoing_nodes.1), channel_id=1, source_target_pairs={{0,7},{1,0},{2,1},{3,2},{4,3},{5,4},{6,5},{7,6},{8,15},{9,8},{10,9... | collective-permute-start | bytes 12296 | tf_op jit(solution)/shard_map/ppermute | solution.py:302
  7.2 4.8 %collective-permute-start.2 = (f32[8,128]{1,0:T(8,128)S(1)}, f32[8,128]{1,0:T(8,128)S(1)}, u32[]{:S(2)}, u32[]{:S(2)}) collective-permute-start(f32[8,128]{1,0:T(8,128)S(1)} %outgoing_nodes.1), channel_id=1, source_target_pairs={{0,1},{1,2},{2,3},{3,4},{4,5},{5,6},{6,7},{7,0},{8,9},{9,10},{10,1... | collective-permute-start | bytes 12296 | tf_op jit(solution)/shard_map/ppermute | solution.py:302
  7.2 4.8 %collective-permute-start.1 = (f32[8,128]{1,0:T(8,128)S(1)}, f32[8,128]{1,0:T(8,128)S(1)}, u32[]{:S(2)}, u32[]{:S(2)}) collective-permute-start(f32[8,128]{1,0:T(8,128)S(1)} %outgoing_nodes.1), channel_id=1, source_target_pairs={{0,24},{8,0},{16,8},{24,16},{1,25},{9,1},{17,9},{25,17},{2,26},{10... | collective-permute-start | bytes 12296 | tf_op jit(solution)/shard_map/ppermute | solution.py:302
  9.7 4.5 %collective-permute-start = (f32[8,128]{1,0:T(8,128)S(1)}, f32[8,128]{1,0:T(8,128)S(1)}, u32[]{:S(2)}, u32[]{:S(2)}) collective-permute-start(f32[8,128]{1,0:T(8,128)S(1)} %outgoing_nodes.1), channel_id=1, source_target_pairs={{0,8},{8,16},{16,24},{24,0},{1,9},{9,17},{17,25},{25,1},{2,10},{10... | collective-permute-start | bytes 12296 | tf_op jit(solution)/shard_map/ppermute | solution.py:302
  14.2 0.8 %copy-start = (f32[9,1024]{1,0:T(8,128)S(1)}, f32[9,1024]{1,0:T(8,128)}, u32[]{:S(2)}) copy-start(f32[9,1024]{1,0:T(8,128)} %inverse.3) | copy-start | bytes 110596
  15.0 0.7 %copy-start.2 = (s32[4,1024]{1,0:T(4,128)S(1)}, s32[4,1024]{1,0:T(4,128)}, u32[]{:S(2)}) copy-start(s32[4,1024]{1,0:T(4,128)} %connect.3) | copy-start | bytes 49156
  15.8 9.9 %copy-start.1 = (f32[9,1024]{1,0:T(8,128)S(1)}, f32[9,1024]{1,0:T(8,128)}, u32[]{:S(2)}) copy-start(f32[9,1024]{1,0:T(8,128)} %inverse.3) | copy-start | bytes 110596
  16.2 9.4 %copy-start.3 = (s32[4,1024]{1,0:T(4,128)S(1)}, s32[4,1024]{1,0:T(4,128)}, u32[]{:S(2)}) copy-start(s32[4,1024]{1,0:T(4,128)} %connect.3) | copy-start | bytes 49156
  25.7 0.7 %copy-start.6 = (f32[1024]{0:T(1024)S(1)}, f32[1024]{0:T(1024)}, u32[]{:S(2)}) copy-start(f32[1024]{0:T(1024)} %param.11) | copy-start | bytes 12292
  36.7 0.7 %copy-start.9 = (s32[1,128]{1,0:T(1,128)S(1)}, s32[1,128]{1,0:T(1,128)}, u32[]{:S(2)}) copy-start(s32[1,128]{1,0:T(1,128)} %send.3) | copy-start | bytes 1540

commit v2 on v1

--- a/solution.py
+++ b/solution.py
@@ -63,15 +63,39 @@
     )
 
 
-def send_kernel(coords, direction, send, out, table):
+def send_kernel(
+    coords, direction, send, slots, connect, inverse, weight,
+    out, table, send_out, slots_out, connect_out, inverse_out, weight_out,
+    coords_in, direction_in, arrived,
+):
+    copies = [
+        pltpu.make_async_copy(src, dst, arrived.at[i])
+        for i, (src, dst) in enumerate(
+            (
+                (coords, coords_in),
+                (direction, direction_in),
+                (send, send_out),
+                (slots, slots_out),
+                (connect, connect_out),
+                (inverse, inverse_out),
+                (weight, weight_out),
+            )
+        )
+    ]
+    for copy in copies:
+        copy.start()
     table[...] = jnp.zeros_like(table)
-    table[0:3, :] = coords[...]
-    table[3:6, :] = direction[...]
-    index = spread(send[...])
+    for copy in copies[:3]:
+        copy.wait()
+    table[0:3, :] = coords_in[...]
+    table[3:6, :] = direction_in[...]
+    index = spread(send_out[...])
     low = index & (LANES - 1)
     first = picked(table[:, :LANES], low)
     second = picked(table[:, LANES:], low)
     out[...] = jnp.where(index < LANES, first, second)
+    for copy in copies[3:]:
+        copy.wait()
 
 
 def cofactor(m):
@@ -95,7 +119,7 @@
 
 
 def det_kernel(
-    blocks, coords, direction, got0, got1, got2, got3, connect, inverse, slots,
+    blocks, own_table, near_dom, far_dom, near_sub, far_sub, connect, inverse, slots,
     low_out, jac_out, table,
 ):
     lane = lane_ids()
@@ -103,15 +127,15 @@
     order = marks(slots[...], LANES)
     entry = lax.broadcasted_iota(jnp.int32, (16, LANES), 1).astype(jnp.bfloat16)
     came_at = by_marks(entry, order)[:SUBS].astype(jnp.int32)
+    from_before = group & 1
     arrived = jnp.where(
-        group == 0,
-        got0[...],
-        jnp.where(group == 1, got1[...], jnp.where(group == 2, got2[...], got3[...])),
+        group < 2,
+        jnp.where(from_before != (lax.axis_index("dom") & 1), near_dom[...], far_dom[...]),
+        jnp.where(from_before != (lax.axis_index("sub") & 1), near_sub[...], far_sub[...]),
     )
     ghosts = picked(arrived, came_at)
-    owned = coords.shape[1]
-    table[0:3, :owned] = coords[...]
-    table[3:6, :owned] = direction[...]
+    owned = own_table.shape[1]
+    table[:, :owned] = own_table[...]
     table[:, owned:] = ghosts
     steps = step_lengths()
     tiles = table.shape[1] // LANES
@@ -289,7 +313,7 @@
     found = found[:height] + found[height : 2 * height] + found[2 * height :]
     found = found + own[...]
     for comp in range(3):
-        gradient[:, comp, :] = found[comp * SUBS : comp * SUBS + TRIALS]
+        gradient[comp] = found[comp * SUBS : comp * SUBS + TRIALS]
     total = jnp.sum(back[...], axis=0)
     total = jnp.broadcast_to(total[:, LANES - 1 :], (TRIALS, LANES))
     total = jnp.sum(jnp.where(lane == sub, total, 0.0), axis=0, keepdims=True)
@@ -297,9 +321,13 @@
     low_out[...] = low[:, :TRIALS]
 
 
-def exchanged(tile, axis, sent_by):
+def exchanged(tile, axis):
     count = lax.axis_size(axis)
-    return lax.ppermute(tile, axis, [(i, (i + sent_by) % count) for i in range(count)])
+    near = lax.ppermute(tile, axis, [(i, i ^ 1) for i in range(count)])
+    far = lax.ppermute(
+        tile, axis, [(i, (i + 1 if i % 2 else i - 1) % count) for i in range(count)]
+    )
+    return near, far
 
 
 def per_device(coords, direction, connect, shape_inv, weight, send_node, recv_slot):
@@ -309,54 +337,73 @@
     elems = connect.shape[1]
     blocks = elems // (2 * LANES)
     local = owned + recv_slot.shape[1]
-    f32 = jnp.float32
-    vmem = pltpu.CompilerParams(vmem_limit_bytes=32 * 1024 * 1024)
-    outgoing = pl.pallas_call(
+    f32, i32 = jnp.float32, jnp.int32
+    shaped = jax.ShapeDtypeStruct
+    params = pltpu.CompilerParams(vmem_limit_bytes=32 * 1024 * 1024)
+    hbm = pl.BlockSpec(memory_space=pltpu.HBM)
+    outgoing, table, sends, slots, connect, inverse, heavy = pl.pallas_call(
         send_kernel,
-        out_shape=jax.ShapeDtypeStruct((SUBS, LANES), f32),
-        scratch_shapes=[pltpu.VMEM((SUBS, owned), f32)],
-        compiler_params=vmem,
+        in_specs=[hbm] * 7,
+        out_shape=(
+            shaped((SUBS, LANES), f32),
+            shaped((SUBS, owned), f32),
+            shaped(send_node.shape, i32),
+            shaped(recv_slot.shape, i32),
+            shaped(connect.shape, i32),
+            shaped(shape_inv.shape, f32),
+            shaped((elems // LANES, LANES), f32),
+        ),
+        scratch_shapes=[
+            pltpu.VMEM(coords.shape, f32),
+            pltpu.VMEM(direction.shape, f32),
+            pltpu.SemaphoreType.DMA((7,)),
+        ],
+        compiler_params=params,
         name="outgoing_nodes",
-    )(coords, direction, send_node)
-    came = (
-        exchanged(outgoing, "dom", 1),
-        exchanged(outgoing, "dom", -1),
-        exchanged(outgoing, "sub", 1),
-        exchanged(outgoing, "sub", -1),
-    )
+    )(
+        *(
+            pltpu.with_memory_space_constraint(given, pltpu.HBM)
+            for given in (
+                coords, direction, send_node, recv_slot, connect, shape_inv,
+                weight.reshape(elems // LANES, LANES),
+            )
+        )
+    )
+    near_dom, far_dom = exchanged(outgoing, "dom")
+    near_sub, far_sub = exchanged(outgoing, "sub")
     lows, jac = pl.pallas_call(
         functools.partial(det_kernel, blocks),
         out_shape=(
-            jax.ShapeDtypeStruct((count, LANES), f32),
-            jax.ShapeDtypeStruct((9, SUBS, elems // 2), f32),
+            shaped((count, LANES), f32),
+            shaped((9, SUBS, elems // 2), f32),
         ),
         scratch_shapes=[pltpu.VMEM((SUBS, local), f32)],
-        compiler_params=vmem,
+        compiler_params=params,
         name="jacobian_dets",
-    )(coords, direction, *came, connect, shape_inv, recv_slot)
+    )(table, near_dom, far_dom, near_sub, far_sub, connect, inverse, slots)
     lows = lax.all_to_all(lows.reshape(count, 1, LANES), AXES, 0, 0).reshape(count, LANES)
     own, back, low = pl.pallas_call(
         functools.partial(grad_kernel, blocks, subs, doms),
         out_shape=(
-            jax.ShapeDtypeStruct((3 * SUBS, owned), f32),
-            jax.ShapeDtypeStruct((count, TRIALS, LANES), f32),
-            jax.ShapeDtypeStruct((1, LANES), f32),
+            shaped((3 * SUBS, owned), f32),
+            shaped((count, TRIALS, LANES), f32),
+            shaped((1, LANES), f32),
         ),
-        compiler_params=vmem,
+        compiler_params=params,
         name="element_gradients",
-    )(lows, jac, weight.reshape(elems // LANES, LANES), connect, shape_inv, recv_slot)
+    )(lows, jac, heavy, connect, inverse, slots)
     back = lax.all_to_all(back, AXES, 0, 0)
     gradient, energy, lowest = pl.pallas_call(
         functools.partial(final_kernel, subs, doms, float(elems * count)),
         out_shape=(
-            jax.ShapeDtypeStruct((TRIALS, 3, owned), f32),
-            jax.ShapeDtypeStruct((1, TRIALS), f32),
-            jax.ShapeDtypeStruct((1, TRIALS), f32),
+            shaped((3, TRIALS, owned), f32),
+            shaped((1, TRIALS), f32),
+            shaped((1, TRIALS), f32),
         ),
-        compiler_params=vmem,
+        compiler_params=params,
         name="owner_sums",
-    )(back, own, send_node, low)
-    return gradient, energy.reshape(TRIALS), lowest.reshape(TRIALS)
+    )(back, own, sends, low)
+    return gradient.transpose(1, 0, 2), energy.reshape(TRIALS), lowest.reshape(TRIALS)
 
 
 def solution(mesh):

time: 39 us -> 33 us (0.85)
  local copies, waits for them, and re-layouts: 5.53 us -> 0 us
  waiting for transfers between devices: 4.5 us -> 3.07 us
  Pallas kernels: 2.49 us -> 3.57 us
  starting transfers between devices: 6.94 us -> 7.54 us
  blocking collectives: 18.5 us -> 18 us
    unnamed x21 -> x0, local copies, waits for them, and re-layouts: 5.53 us -> none
    ppermute x4, waiting for transfers between devices: 4.5 us -> 3.07 us  [the longest x2 1.55 us: exchanged(): near = lax.ppermute(tile, axis, [(i, i ^ 1) for i in range(count)])]
    pallas_call x2, Pallas kernels: 0.57 us -> 1.48 us  [the longest x1 0.99 us: per_device(): pl.pallas_call(send_kernel, in_specs=[hbm] * 7, out_shape=(shaped((SUBS,...]
    ppermute x4, starting transfers between devices: 6.94 us -> 7.54 us  [the longest x2 7 us: exchanged(): lax.ppermute(tile, axis, [(i, (i + 1 if i % 2 else i - 1) % count) for i...]
    all_to_all x1, blocking collectives: 9.42 us -> 8.89 us  [per_device(): lax.all_to_all(lows.reshape(count, 1, LANES), AXES, 0, 0)]
where the time goes in v2:
time: 33 us; the launch traced here: 32.8 us
  blocking collectives  18 us (55%)
  starting transfers between devices  7.54 us (23%)
  Pallas kernels  3.57 us (11%)
  waiting for transfers between devices  3.07 us (9%)
  between operations  0.65 us (2%)
    all_to_all x1, blocking collectives, per_device(): back = lax.all_to_all(back, AXES, 0, 0)  9.08 us
    all_to_all x1, blocking collectives, per_device(): lax.all_to_all(lows.reshape(count, 1, LANES), AXES, 0, 0)  8.89 us
    ppermute x2, starting transfers between devices, exchanged(): lax.ppermute(tile, axis, [(i, (i + 1 if i % 2 else i - 1) % count) for i...  7 us
    ppermute x2, waiting for transfers between devices, exchanged(): near = lax.ppermute(tile, axis, [(i, i ^ 1) for i in range(count)])  1.55 us
    ppermute x2, waiting for transfers between devices, exchanged(): lax.ppermute(tile, axis, [(i, (i + 1 if i % 2 else i - 1) % count) for i...  1.52 us
    pallas_call x1, Pallas kernels, per_device(): pl.pallas_call(functools.partial(grad_kernel, blocks, subs, doms), out_sh...  1.27 us
    pallas_call x1, Pallas kernels, per_device(): pl.pallas_call(send_kernel, in_specs=[hbm] * 7, out_shape=(shaped((SUBS,...  0.99 us
    pallas_call x1, Pallas kernels, per_device(): pl.pallas_call(functools.partial(final_kernel, subs, doms, float(elems *...  0.82 us
  transfers between devices with their start and end apart: 4, of which 2 were waited for; matrix products, arithmetic and copies ran while one was open for 0% of the time, Pallas kernels for 0%

profile of v2, /device:TPU:0, one launch (start us, length us, event | category | flops | bytes accessed | tf_op | source)
XLA Modules:
  0.0 32.8 jit_solution(4552777847771292856)
XLA Ops:
  0.6 1.0 %outgoing_nodes.1 = (f32[8,128]{1,0:T(8,128)S(1)}, f32[8,256]{1,0:T(8,128)S(1)}, s32[1,128]{1,0:T(1,128)S(1)}, s32[1,128]{1,0:T(1,128)S(1)}, s32[4,1024]{1,0:T(4...) custom-call(f32[3,256]{1,0:T(4,128)} %coords.1, f32[3,256]{1,0:T(4,128)} %direction.1, s32[1,128]{1,0:T(1,128)} %send.1, ...), custom_call_target="tpu_custom_call" | custom-call | tf_op jit(solution)/shard_map/outgoing_nodes/pallas_call | solution.py:344
  1.6 4.6 %collective-permute-start.3 = (f32[8,128]{1,0:T(8,128)S(1)}, f32[8,128]{1,0:T(8,128)S(1)}, u32[]{:S(2)}, u32[]{:S(2)}) collective-permute-start(f32[8,128]{1,0:T(8,128)S(1)} %get-tuple-element.19), channel_id=1, source_target_pairs={{0,7},{1,2},{2,1},{3,4},{4,3},{5,6},{6,5},{7,0},{8,15},{9,10},{10,... | collective-permute-start | bytes 12296 | tf_op jit(solution)/shard_map/ppermute | solution.py:327
  6.2 0.0 collective-permute-start.2
  6.2 2.4 %collective-permute-start.1 = (f32[8,128]{1,0:T(8,128)S(1)}, f32[8,128]{1,0:T(8,128)S(1)}, u32[]{:S(2)}, u32[]{:S(2)}) collective-permute-start(f32[8,128]{1,0:T(8,128)S(1)} %get-tuple-element.19), channel_id=1, source_target_pairs={{0,24},{8,16},{16,8},{24,0},{1,25},{9,17},{17,9},{25,1},{2,26},{10... | collective-permute-start | bytes 12296 | tf_op jit(solution)/shard_map/ppermute | solution.py:327
  8.6 0.5 %collective-permute-start = (f32[8,128]{1,0:T(8,128)S(1)}, f32[8,128]{1,0:T(8,128)S(1)}, u32[]{:S(2)}, u32[]{:S(2)}) collective-permute-start(f32[8,128]{1,0:T(8,128)S(1)} %get-tuple-element.19), channel_id=1, source_target_pairs={{0,8},{8,0},{16,24},{24,16},{1,9},{9,1},{17,25},{25,17},{2,10},{10... | collective-permute-start | bytes 12296 | tf_op jit(solution)/shard_map/ppermute | solution.py:326
  9.2 0.0 collective-permute-done.3.far_sub
  9.2 0.0 collective-permute-done.2.near_sub
  9.2 1.5 %collective-permute-done.1.far_dom = f32[8,128]{1,0:T(8,128)S(1)} collective-permute-done((f32[8,128]{1,0:T(8,128)S(1)}, f32[8,128]{1,0:T(8,128)S(1)}, u32[]{:S(2)}, u32[]{:S(2)}) %collective-permute-start.1) | collective-permute-done | bytes 4128 | tf_op jit(solution)/shard_map/ppermute | solution.py:327
  10.7 1.5 %collective-permute-done.near_dom = f32[8,128]{1,0:T(8,128)S(1)} collective-permute-done((f32[8,128]{1,0:T(8,128)S(1)}, f32[8,128]{1,0:T(8,128)S(1)}, u32[]{:S(2)}, u32[]{:S(2)}) %collective-permute-start) | collective-permute-done | bytes 4128 | tf_op jit(solution)/shard_map/ppermute | solution.py:326
  12.2 0.5 %jacobian_dets.1 = (f32[32,128]{1,0:T(8,128)S(1)}, f32[9,8,512]{2,1,0:T(8,128)S(1)}) custom-call(f32[8,256]{1,0:T(8,128)S(1)} %get-tuple-element.18.own_table, f32[8,128]{1,0:T(8,128)S(1)} %collective-permute-done.near_dom, f32[8,128]{1,0:T(8,128)S(1)} %collective-permute-done.1.far_dom, f32[8,128]{1,0:T(8,128)S(1)} %collective-permute-done.2.near_sub, ...), custom_call_target="tpu_custom_call" | custom-call | tf_op jit(solution)/shard_map/jacobian_dets/pallas_call | solution.py:374
  12.7 8.9 %all_to_all.10 = f32[32,1,128]{2,1,0:T(1,128)S(1)} all-to-all(f32[32,1,128]{2,1,0:T(1,128)S(1)} %bitcast.9), channel_id=1, replica_groups=mesh['dom'=4,'sub'=8] {'dom','sub'}, dimensions={0} | all-to-all | bytes 32768 | tf_op jit(solution)/shard_map/all_to_all | solution.py:384
  21.6 1.3 %element_gradients.1 = (f32[24,256]{1,0:T(8,128)S(1)}, f32[32,4,128]{2,1,0:T(4,128)S(1)}, f32[1,128]{1,0:T(1,128)S(1)}) custom-call(f32[32,128]{1,0:T(8,128)S(1)} %bitcast.8, f32[9,8,512]{2,1,0:T(8,128)S(1)} %get-tuple-element.24.jac_in, f32[8,128]{1,0:T(8,128)S(1)} %get-tuple-element.25.weight, s32[4,1024]{1,0:T(4,128)S(1)} %get-tuple-element.20.connect, ...), custom_call_target="tpu_custom_call" | custom-call | tf_op jit(solution)/shard_map/element_gradients/pallas_call | solution.py:385
  22.9 9.1 %all_to_all.11.back = f32[32,4,128]{2,1,0:T(4,128)S(1)} all-to-all(f32[32,4,128]{2,1,0:T(4,128)S(1)} %get-tuple-element.26), channel_id=1, replica_groups=mesh['dom'=4,'sub'=8] {'dom','sub'}, dimensions={0} | all-to-all | bytes 131072 | tf_op jit(solution)/shard_map/all_to_all | solution.py:395
  32.0 0.8 %owner_sums.1 = (f32[3,4,256]{2,1,0:T(4,128)}, f32[1,4]{1,0:T(1,128)}, f32[1,4]{1,0:T(1,128)}) custom-call(f32[32,4,128]{2,1,0:T(4,128)S(1)} %all_to_all.11.back, f32[24,256]{1,0:T(8,128)S(1)} %get-tuple-element.27.own, s32[1,128]{1,0:T(1,128)S(1)} %get-tuple-element.28.send, f32[1,128]{1,0:T(1,128)S(1)} %get-tuple-element.29.low), custom_call_target="tpu_custom_call" | custom-call | tf_op jit(solution)/shard_map/owner_sums/pallas_call | solution.py:396
Async XLA Ops:
  1.6 7.5 %collective-permute-start.3 = (f32[8,128]{1,0:T(8,128)S(1)}, f32[8,128]{1,0:T(8,128)S(1)}, u32[]{:S(2)}, u32[]{:S(2)}) collective-permute-start(f32[8,128]{1,0:T(8,128)S(1)} %get-tuple-element.19), channel_id=1, source_target_pairs={{0,7},{1,2},{2,1},{3,4},{4,3},{5,6},{6,5},{7,0},{8,15},{9,10},{10,... | collective-permute-start | bytes 12296 | tf_op jit(solution)/shard_map/ppermute | solution.py:327
  6.2 3.0 %collective-permute-start.2 = (f32[8,128]{1,0:T(8,128)S(1)}, f32[8,128]{1,0:T(8,128)S(1)}, u32[]{:S(2)}, u32[]{:S(2)}) collective-permute-start(f32[8,128]{1,0:T(8,128)S(1)} %get-tuple-element.19), channel_id=1, source_target_pairs={{0,1},{1,0},{2,3},{3,2},{4,5},{5,4},{6,7},{7,6},{8,9},{9,8},{10,11... | collective-permute-start | bytes 12296 | tf_op jit(solution)/shard_map/ppermute | solution.py:326
  6.2 4.5 %collective-permute-start.1 = (f32[8,128]{1,0:T(8,128)S(1)}, f32[8,128]{1,0:T(8,128)S(1)}, u32[]{:S(2)}, u32[]{:S(2)}) collective-permute-start(f32[8,128]{1,0:T(8,128)S(1)} %get-tuple-element.19), channel_id=1, source_target_pairs={{0,24},{8,16},{16,8},{24,0},{1,25},{9,17},{17,9},{25,1},{2,26},{10... | collective-permute-start | bytes 12296 | tf_op jit(solution)/shard_map/ppermute | solution.py:327
  8.6 3.6 %collective-permute-start = (f32[8,128]{1,0:T(8,128)S(1)}, f32[8,128]{1,0:T(8,128)S(1)}, u32[]{:S(2)}, u32[]{:S(2)}) collective-permute-start(f32[8,128]{1,0:T(8,128)S(1)} %get-tuple-element.19), channel_id=1, source_target_pairs={{0,8},{8,0},{16,24},{24,16},{1,9},{9,1},{17,25},{25,17},{2,10},{10... | collective-permute-start | bytes 12296 | tf_op jit(solution)/shard_map/ppermute | solution.py:326

commit v3 on v2

--- a/solution.py
+++ b/solution.py
@@ -57,35 +57,36 @@
     return jnp.where(hit, 1.0, 0.0).astype(jnp.bfloat16)
 
 
+def column_marks(column, count):
+    shape = (column.shape[0], count)
+    places = lax.broadcasted_iota(jnp.int32, shape, 1)
+    hit = places == jnp.broadcast_to(column, shape)
+    return jnp.where(hit, 1.0, 0.0).astype(jnp.bfloat16)
+
+
 def by_marks(left, right):
     return lax.dot_general(
         left, right, (((1,), (1,)), ((), ())), preferred_element_type=jnp.float32
     )
 
 
-def send_kernel(
-    coords, direction, send, slots, connect, inverse, weight,
-    out, table, send_out, slots_out, connect_out, inverse_out, weight_out,
-    coords_in, direction_in, arrived,
-):
+def fetch(pairs, arrived):
     copies = [
-        pltpu.make_async_copy(src, dst, arrived.at[i])
-        for i, (src, dst) in enumerate(
-            (
-                (coords, coords_in),
-                (direction, direction_in),
-                (send, send_out),
-                (slots, slots_out),
-                (connect, connect_out),
-                (inverse, inverse_out),
-                (weight, weight_out),
-            )
-        )
+        pltpu.make_async_copy(src, dst, arrived.at[i]) for i, (src, dst) in enumerate(pairs)
     ]
     for copy in copies:
         copy.start()
+    return copies
+
+
+def send_kernel(
+    coords, direction, send, out, table, send_out, coords_in, direction_in, arrived
+):
+    copies = fetch(
+        ((coords, coords_in), (direction, direction_in), (send, send_out)), arrived
+    )
     table[...] = jnp.zeros_like(table)
-    for copy in copies[:3]:
+    for copy in copies:
         copy.wait()
     table[0:3, :] = coords_in[...]
     table[3:6, :] = direction_in[...]
@@ -94,8 +95,58 @@
     first = picked(table[:, :LANES], low)
     second = picked(table[:, LANES:], low)
     out[...] = jnp.where(index < LANES, first, second)
-    for copy in copies[3:]:
-        copy.wait()
+
+
+def prepare_kernel(
+    blocks, slots, connect, inverse, weight,
+    came_out, slots_out, index_out, inverse_out, weight_out, marks_out,
+    connect_in, inverse_in, weight_in, arrived,
+):
+    copies = fetch(
+        (
+            (connect, connect_in),
+            (slots, slots_out),
+            (weight, weight_in),
+            (inverse, inverse_in),
+        ),
+        arrived,
+    )
+    copies[0].wait()
+    width = blocks * LANES
+    for corner in range(4):
+        for block in range(blocks):
+            index_out[corner, :, block * LANES : (block + 1) * LANES] = halves(
+                connect_in, corner, block, blocks
+            )
+    nodes = marks_out.shape[2]
+    for half in range(2):
+        for block in range(blocks):
+            start = half * width + block * LANES
+            columns = jnp.transpose(
+                jnp.concatenate([connect_in[:, start : start + LANES]] * 2, axis=0)
+            )
+            for corner in range(4):
+                row = corner * width + block * LANES
+                marks_out[half, row : row + LANES, :] = column_marks(
+                    columns[:, corner : corner + 1], nodes
+                )
+    copies[1].wait()
+    order = marks(slots_out[...], LANES)
+    entry = lax.broadcasted_iota(jnp.int32, (16, LANES), 1).astype(jnp.bfloat16)
+    came_out[...] = by_marks(entry, order)[:SUBS].astype(jnp.int32)
+    copies[2].wait()
+    for block in range(blocks):
+        weight_out[:, block * LANES : (block + 1) * LANES] = jnp.where(
+            sub_ids() < TRIALS,
+            spread(weight_in[block : block + 1, :]),
+            spread(weight_in[blocks + block : blocks + block + 1, :]),
+        )
+    copies[3].wait()
+    for row in range(9):
+        for block in range(blocks):
+            inverse_out[row, :, block * LANES : (block + 1) * LANES] = halves(
+                inverse_in, row, block, blocks
+            )
 
 
 def cofactor(m):
@@ -119,21 +170,22 @@
 
 
 def det_kernel(
-    blocks, own_table, near_dom, far_dom, near_sub, far_sub, connect, inverse, slots,
+    blocks, orders, own_table, came3, came2, came1, came0, connect, inverse, came_at,
     low_out, jac_out, table,
 ):
     lane = lane_ids()
     group = lane // 32
-    order = marks(slots[...], LANES)
-    entry = lax.broadcasted_iota(jnp.int32, (16, LANES), 1).astype(jnp.bfloat16)
-    came_at = by_marks(entry, order)[:SUBS].astype(jnp.int32)
+    came = (came0, came1, came2, came3)
+    near_dom, far_dom, near_sub, far_sub = (
+        tile_of(kind, orders, came) for kind in ("near_dom", "far_dom", "near_sub", "far_sub")
+    )
     from_before = group & 1
     arrived = jnp.where(
         group < 2,
-        jnp.where(from_before != (lax.axis_index("dom") & 1), near_dom[...], far_dom[...]),
-        jnp.where(from_before != (lax.axis_index("sub") & 1), near_sub[...], far_sub[...]),
-    )
-    ghosts = picked(arrived, came_at)
+        jnp.where(from_before != (lax.axis_index("dom") & 1), near_dom, far_dom),
+        jnp.where(from_before != (lax.axis_index("sub") & 1), near_sub, far_sub),
+    )
+    ghosts = picked(arrived, came_at[...])
     owned = own_table.shape[1]
     table[:, :owned] = own_table[...]
     table[:, owned:] = ghosts
@@ -149,9 +201,10 @@
     ]
     lowest = None
     for block in range(blocks):
+        cut = slice(block * LANES, (block + 1) * LANES)
         corners = []
         for corner in range(4):
-            index = halves(connect, corner, block, blocks)
+            index = connect[corner, :, cut]
             low = index & (LANES - 1)
             in_first = index < LANES
             in_second = index < 2 * LANES
@@ -169,7 +222,7 @@
                     for comp in range(3)
                 ]
             )
-        weights = [halves(inverse, row, block, blocks) for row in range(9)]
+        weights = [inverse[row, :, cut] for row in range(9)]
         jac = []
         for comp in range(3):
             edges = [corners[k][comp] - corners[0][comp] for k in (1, 2, 3)]
@@ -186,7 +239,7 @@
         lowest = det if lowest is None else jnp.minimum(lowest, det)
         for comp in range(3):
             for col in range(3):
-                jac_out[3 * comp + col, :, block * LANES : (block + 1) * LANES] = jac[comp][col]
+                jac_out[3 * comp + col, :, cut] = jac[comp][col]
     least = spread_lanes(jnp.min(lowest, axis=1, keepdims=True))
     at_trial = jnp.where(lane == (sub_ids() & (TRIALS - 1)), least, jnp.inf)
     row = jnp.min(at_trial, axis=0, keepdims=True)
@@ -198,14 +251,13 @@
 
 
 def grad_kernel(
-    blocks, sub_count, dom_count, lows, jac_in, weight, connect, inverse, slots,
+    blocks, sub_count, dom_count, lows, jac_in, weight, spots, inverse, slots,
     own_out, back_out, low_out,
 ):
     lane, sub = lane_ids(), sub_ids()
     lowest_row = jnp.min(lows[...], axis=0, keepdims=True)
     low_out[...] = lowest_row
-    mine = jnp.where(lane == (sub & (TRIALS - 1)), spread(lowest_row), 0.0)
-    lowest = spread_lanes(jnp.sum(mine, axis=1, keepdims=True))
+    lowest = picked(spread(lowest_row), sub & (TRIALS - 1))
     shift = lowest - 1.0 - jnp.abs(lowest)
     energy = None
     terms = [[[] for _ in range(3)] for _ in range(4)]
@@ -221,17 +273,13 @@
                     squares = squares + jac[comp][col] * jac[comp][col]
         lifted = det - shift
         power = jnp.exp(jnp.log(lifted) * (-2.0 / 3.0))
-        heavy = jnp.where(
-            sub < TRIALS,
-            spread(weight[block : block + 1, :]),
-            spread(weight[blocks + block : blocks + block + 1, :]),
-        )
+        heavy = weight[:, cut]
         scaled = heavy * power
         part = scaled * squares
         energy = part if energy is None else energy + part
         scale_jac = scaled * (2.0 / 3.0)
         scale_cof = part / lifted * (2.0 / 9.0)
-        weights = [halves(inverse, row, block, blocks) for row in range(9)]
+        weights = [inverse[row, :, cut] for row in range(9)]
         for comp in range(3):
             djac = [scale_jac * jac[comp][col] - scale_cof * cofac[comp][col] for col in range(3)]
             edges = [
@@ -241,18 +289,18 @@
             terms[0][comp].append(-(edges[0] + edges[1] + edges[2]))
             for k in range(3):
                 terms[k + 1][comp].append(edges[k])
-    width = blocks * LANES
     local = own_out.shape[1] + LANES
-    sums = [None, None]
-    for corner in range(4):
-        values = jnp.concatenate(
-            [jnp.concatenate(terms[corner][comp], axis=1) for comp in range(3)], axis=0
-        )
-        left = jnp.concatenate(split_three(values), axis=0)
-        for half in range(2):
-            row = connect[corner : corner + 1, half * width : (half + 1) * width]
-            found = by_marks(left, marks(row, local))
-            sums[half] = found if sums[half] is None else sums[half] + found
+    values = jnp.concatenate(
+        [
+            jnp.concatenate([part for corner in terms for part in corner[comp]], axis=1)
+            for comp in range(3)
+        ],
+        axis=0,
+    )
+    left = jnp.concatenate(split_three(values), axis=0)
+    sums = [
+        jnp.dot(left, spots[half], preferred_element_type=jnp.float32) for half in range(2)
+    ]
     rows = 3 * SUBS
     sums = [s[:rows] + s[rows : 2 * rows] + s[2 * rows :] for s in sums]
     upper = lax.broadcasted_iota(jnp.int32, (SUBS, local), 0) < TRIALS
@@ -321,13 +369,51 @@
     low_out[...] = low[:, :TRIALS]
 
 
-def exchanged(tile, axis):
-    count = lax.axis_size(axis)
-    near = lax.ppermute(tile, axis, [(i, i ^ 1) for i in range(count)])
-    far = lax.ppermute(
-        tile, axis, [(i, (i + 1 if i % 2 else i - 1) % count) for i in range(count)]
-    )
-    return near, far
+def partner(kind, doms, subs, dom, sub):
+    if kind == "near_dom":
+        return (dom ^ 1) * subs + sub
+    if kind == "far_dom":
+        return ((dom + 1 if dom % 2 else dom - 1) % doms) * subs + sub
+    if kind == "near_sub":
+        return dom * subs + (sub ^ 1)
+    return dom * subs + (sub + 1 if sub % 2 else sub - 1) % subs
+
+
+def exchanges(subs):
+    usual = ("far_dom", "far_sub", "near_dom", "near_sub")
+    last = ("near_sub", "far_sub", "far_dom", "near_dom")
+    return [last if sub >= subs else usual for sub in range(subs)]
+
+
+def exchanged(tile, doms, subs):
+    orders = exchanges(subs)
+    return [
+        lax.ppermute(
+            tile,
+            AXES,
+            [
+                (dom * subs + sub, partner(orders[sub][step], doms, subs, dom, sub))
+                for dom in range(doms)
+                for sub in range(subs)
+            ],
+        )
+        for step in range(4)
+    ]
+
+
+def tile_of(kind, orders, came):
+    sub = lax.axis_index("sub")
+    tile = None
+    for step in range(4):
+        places = [place for place, order in enumerate(orders) if order[step] == kind]
+        if not places:
+            continue
+        if tile is None:
+            tile = came[step][...]
+            continue
+        here = functools.reduce(jnp.logical_or, [sub == place for place in places])
+        tile = jnp.where(here, came[step][...], tile)
+    return tile
 
 
 def per_device(coords, direction, connect, shape_inv, weight, send_node, recv_slot):
@@ -341,38 +427,50 @@
     shaped = jax.ShapeDtypeStruct
     params = pltpu.CompilerParams(vmem_limit_bytes=32 * 1024 * 1024)
     hbm = pl.BlockSpec(memory_space=pltpu.HBM)
-    outgoing, table, sends, slots, connect, inverse, heavy = pl.pallas_call(
+
+    def pinned(*arrays):
+        return [pltpu.with_memory_space_constraint(x, pltpu.HBM) for x in arrays]
+
+    outgoing, table, sends = pl.pallas_call(
         send_kernel,
-        in_specs=[hbm] * 7,
+        in_specs=[hbm] * 3,
         out_shape=(
             shaped((SUBS, LANES), f32),
             shaped((SUBS, owned), f32),
             shaped(send_node.shape, i32),
-            shaped(recv_slot.shape, i32),
-            shaped(connect.shape, i32),
-            shaped(shape_inv.shape, f32),
-            shaped((elems // LANES, LANES), f32),
         ),
         scratch_shapes=[
             pltpu.VMEM(coords.shape, f32),
             pltpu.VMEM(direction.shape, f32),
-            pltpu.SemaphoreType.DMA((7,)),
+            pltpu.SemaphoreType.DMA((3,)),
         ],
         compiler_params=params,
         name="outgoing_nodes",
-    )(
-        *(
-            pltpu.with_memory_space_constraint(given, pltpu.HBM)
-            for given in (
-                coords, direction, send_node, recv_slot, connect, shape_inv,
-                weight.reshape(elems // LANES, LANES),
-            )
-        )
-    )
-    near_dom, far_dom = exchanged(outgoing, "dom")
-    near_sub, far_sub = exchanged(outgoing, "sub")
+    )(*pinned(coords, direction, send_node))
+    came_at, slots, index, inverse, heavy, spots = pl.pallas_call(
+        functools.partial(prepare_kernel, blocks),
+        in_specs=[hbm] * 4,
+        out_shape=(
+            shaped((SUBS, LANES), i32),
+            shaped(recv_slot.shape, i32),
+            shaped((4, SUBS, elems // 2), i32),
+            shaped((9, SUBS, elems // 2), f32),
+            shaped((SUBS, elems // 2), f32),
+            shaped((2, 2 * elems, local), jnp.bfloat16),
+        ),
+        scratch_shapes=[
+            pltpu.VMEM(connect.shape, i32),
+            pltpu.VMEM(shape_inv.shape, f32),
+            pltpu.VMEM((elems // LANES, LANES), f32),
+            pltpu.SemaphoreType.DMA((4,)),
+        ],
+        compiler_params=params,
+        cost_estimate=pl.CostEstimate(flops=1000000, bytes_accessed=4000000, transcendentals=0),
+        name="prepared_elements",
+    )(*pinned(recv_slot, connect, shape_inv, weight.reshape(elems // LANES, LANES)))
+    came = exchanged(outgoing, doms, subs)
     lows, jac = pl.pallas_call(
-        functools.partial(det_kernel, blocks),
+        functools.partial(det_kernel, blocks, exchanges(subs)),
         out_shape=(
             shaped((count, LANES), f32),
             shaped((9, SUBS, elems // 2), f32),
@@ -380,7 +478,7 @@
         scratch_shapes=[pltpu.VMEM((SUBS, local), f32)],
         compiler_params=params,
         name="jacobian_dets",
-    )(table, near_dom, far_dom, near_sub, far_sub, connect, inverse, slots)
+    )(table, *came[::-1], index, inverse, came_at)
     lows = lax.all_to_all(lows.reshape(count, 1, LANES), AXES, 0, 0).reshape(count, LANES)
     own, back, low = pl.pallas_call(
         functools.partial(grad_kernel, blocks, subs, doms),
@@ -391,7 +489,7 @@
         ),
         compiler_params=params,
         name="element_gradients",
-    )(lows, jac, heavy, connect, inverse, slots)
+    )(lows, jac, heavy, spots, inverse, slots)
     back = lax.all_to_all(back, AXES, 0, 0)
     gradient, energy, lowest = pl.pallas_call(
         functools.partial(final_kernel, subs, doms, float(elems * count)),

time: 33 us -> 32.1 us (0.973)
  waiting for transfers between devices: 3.07 us -> 1.18 us
  Pallas kernels: 3.57 us -> 4.79 us
    ppermute x4, waiting for transfers between devices: 3.07 us -> 1.18 us  [exchanged(): lax.ppermute(tile, AXES, [(dom * subs + sub, partner(orders[sub][step], d...]
    pallas_call x2 -> x3, Pallas kernels: 1.48 us -> 3.1 us  [the longest x1 1.87 us: per_device(): pl.pallas_call(functools.partial(prepare_kernel, blocks), in_specs=[hbm]...]
    pallas_call x1, Pallas kernels: 1.27 us -> 0.87 us  [per_device(): pl.pallas_call(functools.partial(grad_kernel, blocks, subs, doms), out_sh...]
  transfers between devices with their start and end apart: 4 -> 4, of which waited for: 2 -> 1; matrix products, arithmetic and copies ran while one was open for 0% -> 0% of each run, Pallas kernels for 0% -> 6%
where the time goes in v3:
time: 32.1 us; the launch traced here: 31.8 us
  blocking collectives  17.9 us (56%)
  starting transfers between devices  7.26 us (23%)
  Pallas kernels  4.79 us (15%)
  waiting for transfers between devices  1.18 us (4%)
  between operations  0.67 us (2%)
    all_to_all x1, blocking collectives, per_device(): back = lax.all_to_all(back, AXES, 0, 0)  9.08 us
    all_to_all x1, blocking collectives, per_device(): lax.all_to_all(lows.reshape(count, 1, LANES), AXES, 0, 0)  8.83 us
    ppermute x4, starting transfers between devices, exchanged(): lax.ppermute(tile, AXES, [(dom * subs + sub, partner(orders[sub][step], d...  7.26 us
    pallas_call x1, Pallas kernels, per_device(): pl.pallas_call(functools.partial(prepare_kernel, blocks), in_specs=[hbm]...  1.87 us
    ppermute x4, waiting for transfers between devices, exchanged(): lax.ppermute(tile, AXES, [(dom * subs + sub, partner(orders[sub][step], d...  1.18 us
    pallas_call x1, Pallas kernels, per_device(): pl.pallas_call(functools.partial(grad_kernel, blocks, subs, doms), out_sh...  0.87 us
    pallas_call x1, Pallas kernels, per_device(): pl.pallas_call(functools.partial(final_kernel, subs, doms, float(elems *...  0.82 us
    pallas_call x1, Pallas kernels, per_device(): pl.pallas_call(send_kernel, in_specs=[hbm] * 3, out_shape=(shaped((SUBS,...  0.81 us
  transfers between devices with their start and end apart: 4, of which 1 were waited for; matrix products, arithmetic and copies ran while one was open for 0% of the time, Pallas kernels for 6%

profile of v3, /device:TPU:0, one launch (start us, length us, event | category | flops | bytes accessed | tf_op | source)
XLA Modules:
  0.0 31.8 jit_solution(7645536432181246341)
XLA Ops:
  0.6 0.8 %outgoing_nodes.1 = (f32[8,128]{1,0:T(8,128)S(1)}, f32[8,256]{1,0:T(8,128)S(1)}, s32[1,128]{1,0:T(1,128)S(1)}) custom-call(f32[3,256]{1,0:T(4,128)} %coords.1, f32[3,256]{1,0:T(4,128)} %direction.1, s32[1,128]{1,0:T(1,128)} %send.1), custom_call_target="tpu_custom_call" | custom-call | tf_op jit(solution)/shard_map/outgoing_nodes/pallas_call | solution.py:434
  1.4 4.0 %collective-permute-start.3 = (f32[8,128]{1,0:T(8,128)S(1)}, f32[8,128]{1,0:T(8,128)S(1)}, u32[]{:S(2)}, u32[]{:S(2)}) collective-permute-start(f32[8,128]{1,0:T(8,128)S(1)} %get-tuple-element.21), channel_id=1, source_target_pairs={{0,24},{1,25},{2,26},{3,27},{4,28},{5,29},{6,30},{7,31},{8,16},{9,... | collective-permute-start | bytes 12296 | tf_op jit(solution)/shard_map/ppermute | solution.py:391
  5.4 2.8 %collective-permute-start.2 = (f32[8,128]{1,0:T(8,128)S(1)}, f32[8,128]{1,0:T(8,128)S(1)}, u32[]{:S(2)}, u32[]{:S(2)}) collective-permute-start(f32[8,128]{1,0:T(8,128)S(1)} %get-tuple-element.21), channel_id=1, source_target_pairs={{0,7},{1,2},{2,1},{3,4},{4,3},{5,6},{6,5},{7,0},{8,15},{9,10},{10,... | collective-permute-start | bytes 12296 | tf_op jit(solution)/shard_map/ppermute | solution.py:391
  8.2 0.5 %collective-permute-start.1 = (f32[8,128]{1,0:T(8,128)S(1)}, f32[8,128]{1,0:T(8,128)S(1)}, u32[]{:S(2)}, u32[]{:S(2)}) collective-permute-start(f32[8,128]{1,0:T(8,128)S(1)} %get-tuple-element.21), channel_id=1, source_target_pairs={{0,8},{1,9},{2,10},{3,11},{4,12},{5,13},{6,14},{7,15},{8,0},{9,1},... | collective-permute-start | bytes 12296 | tf_op jit(solution)/shard_map/ppermute | solution.py:391
  8.7 0.0 collective-permute-start
  8.7 1.9 %prepared_elements.1 = (s32[8,128]{1,0:T(8,128)S(1)}, s32[1,128]{1,0:T(1,128)S(1)}, s32[4,8,512]{2,1,0:T(8,128)S(1)}, f32[9,8,512]{2,1,0:T(8,128)S(1)}, f32[8,51...) custom-call(s32[1,128]{1,0:T(1,128)} %slots.1, s32[4,1024]{1,0:T(4,128)} %connect.1, f32[9,1024]{1,0:T(8,128)} %inverse.1, ...), custom_call_target="tpu_custom_call" | custom-call | flops 1000000 | bytes 4000000 | tf_op jit(solution)/shard_map/prepared_elements/pallas_call | solution.py:450
  10.6 0.0 collective-permute-done.3.came0
  10.6 0.0 collective-permute-done.2.came1
  10.6 1.2 %collective-permute-done.1.came2 = f32[8,128]{1,0:T(8,128)S(1)} collective-permute-done((f32[8,128]{1,0:T(8,128)S(1)}, f32[8,128]{1,0:T(8,128)S(1)}, u32[]{:S(2)}, u32[]{:S(2)}) %collective-permute-start.1) | collective-permute-done | bytes 4128 | tf_op jit(solution)/shard_map/ppermute | solution.py:391
  11.8 0.0 collective-permute-done.came3
  11.8 0.4 %jacobian_dets.1 = (f32[32,128]{1,0:T(8,128)S(1)}, f32[9,8,512]{2,1,0:T(8,128)S(1)}) custom-call(f32[8,256]{1,0:T(8,128)S(1)} %get-tuple-element.20.own_table, f32[8,128]{1,0:T(8,128)S(1)} %collective-permute-done.came3, f32[8,128]{1,0:T(8,128)S(1)} %collective-permute-done.1.came2, f32[8,128]{1,0:T(8,128)S(1)} %collective-permute-done.2.came1, ...), custom_call_target="tpu_custom_call" | custom-call | tf_op jit(solution)/shard_map/jacobian_dets/pallas_call | solution.py:472
  12.2 8.8 %all_to_all.10 = f32[32,1,128]{2,1,0:T(1,128)S(1)} all-to-all(f32[32,1,128]{2,1,0:T(1,128)S(1)} %bitcast.9), channel_id=1, replica_groups=mesh['dom'=4,'sub'=8] {'dom','sub'}, dimensions={0} | all-to-all | bytes 32768 | tf_op jit(solution)/shard_map/all_to_all | solution.py:482
  21.0 0.9 %element_gradients.1 = (f32[24,256]{1,0:T(8,128)S(1)}, f32[32,4,128]{2,1,0:T(4,128)S(1)}, f32[1,128]{1,0:T(1,128)S(1)}) custom-call(f32[32,128]{1,0:T(8,128)S(1)} %bitcast.8, f32[9,8,512]{2,1,0:T(8,128)S(1)} %get-tuple-element.26.jac_in, f32[8,512]{1,0:T(8,128)S(1)} %get-tuple-element.27.weight, bf16[2,2048,384]{2,1,0:T(8,128)(2,1)S(1)} %get-tuple-element.28.spots, ...), custom_call_target="tpu_custom_call" | custom-call | tf_op jit(solution)/shard_map/element_gradients/pallas_call | solution.py:483
  21.9 9.1 %all_to_all.11.back = f32[32,4,128]{2,1,0:T(4,128)S(1)} all-to-all(f32[32,4,128]{2,1,0:T(4,128)S(1)} %get-tuple-element.30), channel_id=1, replica_groups=mesh['dom'=4,'sub'=8] {'dom','sub'}, dimensions={0} | all-to-all | bytes 131072 | tf_op jit(solution)/shard_map/all_to_all | solution.py:493
  31.0 0.8 %owner_sums.1 = (f32[3,4,256]{2,1,0:T(4,128)}, f32[1,4]{1,0:T(1,128)}, f32[1,4]{1,0:T(1,128)}) custom-call(f32[32,4,128]{2,1,0:T(4,128)S(1)} %all_to_all.11.back, f32[24,256]{1,0:T(8,128)S(1)} %get-tuple-element.31.own, s32[1,128]{1,0:T(1,128)S(1)} %get-tuple-element.32.send, f32[1,128]{1,0:T(1,128)S(1)} %get-tuple-element.33.low), custom_call_target="tpu_custom_call" | custom-call | tf_op jit(solution)/shard_map/owner_sums/pallas_call | solution.py:494
Async XLA Ops:
  1.4 9.1 %collective-permute-start.3 = (f32[8,128]{1,0:T(8,128)S(1)}, f32[8,128]{1,0:T(8,128)S(1)}, u32[]{:S(2)}, u32[]{:S(2)}) collective-permute-start(f32[8,128]{1,0:T(8,128)S(1)} %get-tuple-element.21), channel_id=1, source_target_pairs={{0,24},{1,25},{2,26},{3,27},{4,28},{5,29},{6,30},{7,31},{8,16},{9,... | collective-permute-start | bytes 12296 | tf_op jit(solution)/shard_map/ppermute | solution.py:391
  5.4 5.2 %collective-permute-start.2 = (f32[8,128]{1,0:T(8,128)S(1)}, f32[8,128]{1,0:T(8,128)S(1)}, u32[]{:S(2)}, u32[]{:S(2)}) collective-permute-start(f32[8,128]{1,0:T(8,128)S(1)} %get-tuple-element.21), channel_id=1, source_target_pairs={{0,7},{1,2},{2,1},{3,4},{4,3},{5,6},{6,5},{7,0},{8,15},{9,10},{10,... | collective-permute-start | bytes 12296 | tf_op jit(solution)/shard_map/ppermute | solution.py:391
  8.2 3.6 %collective-permute-start.1 = (f32[8,128]{1,0:T(8,128)S(1)}, f32[8,128]{1,0:T(8,128)S(1)}, u32[]{:S(2)}, u32[]{:S(2)}) collective-permute-start(f32[8,128]{1,0:T(8,128)S(1)} %get-tuple-element.21), channel_id=1, source_target_pairs={{0,8},{1,9},{2,10},{3,11},{4,12},{5,13},{6,14},{7,15},{8,0},{9,1},... | collective-permute-start | bytes 12296 | tf_op jit(solution)/shard_map/ppermute | solution.py:391
  8.7 3.1 %collective-permute-start = (f32[8,128]{1,0:T(8,128)S(1)}, f32[8,128]{1,0:T(8,128)S(1)}, u32[]{:S(2)}, u32[]{:S(2)}) collective-permute-start(f32[8,128]{1,0:T(8,128)S(1)} %get-tuple-element.21), channel_id=1, source_target_pairs={{0,1},{1,0},{2,3},{3,2},{4,5},{5,4},{6,7},{7,6},{8,9},{9,8},{10,11... | collective-permute-start | bytes 12296 | tf_op jit(solution)/shard_map/ppermute | solution.py:391

commit v4 on v3

--- a/solution.py
+++ b/solution.py
@@ -34,6 +34,14 @@
     return jnp.where(
         trial == 0, 1.0, jnp.where(trial == 1, 0.5, jnp.where(trial == 2, 0.25, 0.125))
     ).astype(jnp.float32)
+
+
+def trial_places(table, tile, steps):
+    cut = slice(tile * LANES, (tile + 1) * LANES)
+    return [
+        spread(table[comp : comp + 1, cut]) + steps * spread(table[3 + comp : 4 + comp, cut])
+        for comp in range(3)
+    ]
 
 
 def halves(ref, row, block, blocks):
@@ -98,9 +106,9 @@
 
 
 def prepare_kernel(
-    blocks, slots, connect, inverse, weight,
-    came_out, slots_out, index_out, inverse_out, weight_out, marks_out,
-    connect_in, inverse_in, weight_in, arrived,
+    blocks, table, sends, slots, connect, inverse, weight,
+    came_out, slots_out, index_out, corner_out, inverse_out, weight_out, marks_out,
+    send_marks_out, connect_in, inverse_in, weight_in, arrived,
 ):
     copies = fetch(
         (
@@ -111,13 +119,22 @@
         ),
         arrived,
     )
+    steps = step_lengths()
+    firsts, seconds = trial_places(table, 0, steps), trial_places(table, 1, steps)
+    columns = jnp.transpose(spread(sends[...]))
+    send_marks_out[...] = column_marks(columns[:, :1], send_marks_out.shape[1])
     copies[0].wait()
     width = blocks * LANES
     for corner in range(4):
         for block in range(blocks):
-            index_out[corner, :, block * LANES : (block + 1) * LANES] = halves(
-                connect_in, corner, block, blocks
-            )
+            cut = slice(block * LANES, (block + 1) * LANES)
+            index = halves(connect_in, corner, block, blocks)
+            index_out[corner, :, cut] = index
+            low = index & (LANES - 1)
+            for comp in range(3):
+                corner_out[3 * corner + comp, :, cut] = jnp.where(
+                    index < LANES, picked(firsts[comp], low), picked(seconds[comp], low)
+                )
     nodes = marks_out.shape[2]
     for half in range(2):
         for block in range(blocks):
@@ -126,7 +143,7 @@
                 jnp.concatenate([connect_in[:, start : start + LANES]] * 2, axis=0)
             )
             for corner in range(4):
-                row = corner * width + block * LANES
+                row = (4 * block + corner) * LANES
                 marks_out[half, row : row + LANES, :] = column_marks(
                     columns[:, corner : corner + 1], nodes
                 )
@@ -170,7 +187,7 @@
 
 
 def det_kernel(
-    blocks, orders, own_table, came3, came2, came1, came0, connect, inverse, came_at,
+    blocks, orders, corner_in, came3, came2, came1, came0, connect, inverse, came_at,
     low_out, jac_out, table,
 ):
     lane = lane_ids()
@@ -185,20 +202,9 @@
         jnp.where(from_before != (lax.axis_index("dom") & 1), near_dom, far_dom),
         jnp.where(from_before != (lax.axis_index("sub") & 1), near_sub, far_sub),
     )
-    ghosts = picked(arrived, came_at[...])
-    owned = own_table.shape[1]
-    table[:, :owned] = own_table[...]
-    table[:, owned:] = ghosts
-    steps = step_lengths()
-    tiles = table.shape[1] // LANES
-    places = [
-        [
-            spread(table[comp : comp + 1, tile * LANES : (tile + 1) * LANES])
-            + steps * spread(table[3 + comp : 4 + comp, tile * LANES : (tile + 1) * LANES])
-            for tile in range(tiles)
-        ]
-        for comp in range(3)
-    ]
+    table[...] = picked(arrived, came_at[...])
+    ghosts = trial_places(table, 0, step_lengths())
+    owned = 2 * LANES
     lowest = None
     for block in range(blocks):
         cut = slice(block * LANES, (block + 1) * LANES)
@@ -206,18 +212,12 @@
         for corner in range(4):
             index = connect[corner, :, cut]
             low = index & (LANES - 1)
-            in_first = index < LANES
-            in_second = index < 2 * LANES
             corners.append(
                 [
                     jnp.where(
-                        in_first,
-                        picked(places[comp][0], low),
-                        jnp.where(
-                            in_second,
-                            picked(places[comp][1], low),
-                            picked(places[comp][2], low),
-                        ),
+                        index < owned,
+                        corner_in[3 * corner + comp, :, cut],
+                        picked(ghosts[comp], low),
                     )
                     for comp in range(3)
                 ]
@@ -260,7 +260,7 @@
     lowest = picked(spread(lowest_row), sub & (TRIALS - 1))
     shift = lowest - 1.0 - jnp.abs(lowest)
     energy = None
-    terms = [[[] for _ in range(3)] for _ in range(4)]
+    sums = [None, None]
     for block in range(blocks):
         cut = slice(block * LANES, (block + 1) * LANES)
         jac = [[jac_in[3 * comp + col, :, cut] for col in range(3)] for comp in range(3)]
@@ -280,27 +280,22 @@
         scale_jac = scaled * (2.0 / 3.0)
         scale_cof = part / lifted * (2.0 / 9.0)
         weights = [inverse[row, :, cut] for row in range(9)]
+        terms = []
         for comp in range(3):
             djac = [scale_jac * jac[comp][col] - scale_cof * cofac[comp][col] for col in range(3)]
             edges = [
                 djac[0] * weights[3 * k] + djac[1] * weights[3 * k + 1] + djac[2] * weights[3 * k + 2]
                 for k in range(3)
             ]
-            terms[0][comp].append(-(edges[0] + edges[1] + edges[2]))
-            for k in range(3):
-                terms[k + 1][comp].append(edges[k])
+            terms.append([-(edges[0] + edges[1] + edges[2]), *edges])
+        values = jnp.concatenate([jnp.concatenate(parts, axis=1) for parts in terms], axis=0)
+        left = jnp.concatenate(split_three(values), axis=0)
+        height = 4 * LANES
+        for half in range(2):
+            right = spots[half, block * height : (block + 1) * height, :]
+            found = jnp.dot(left, right, preferred_element_type=jnp.float32)
+            sums[half] = found if block == 0 else sums[half] + found
     local = own_out.shape[1] + LANES
-    values = jnp.concatenate(
-        [
-            jnp.concatenate([part for corner in terms for part in corner[comp]], axis=1)
-            for comp in range(3)
-        ],
-        axis=0,
-    )
-    left = jnp.concatenate(split_three(values), axis=0)
-    sums = [
-        jnp.dot(left, spots[half], preferred_element_type=jnp.float32) for half in range(2)
-    ]
     rows = 3 * SUBS
     sums = [s[:rows] + s[rows : 2 * rows] + s[2 * rows :] for s in sums]
     upper = lax.broadcasted_iota(jnp.int32, (SUBS, local), 0) < TRIALS
@@ -332,7 +327,7 @@
 
 
 def final_kernel(
-    sub_count, dom_count, elem_total, back, own, send, low, gradient, energy_out, low_out
+    sub_count, dom_count, elem_total, back, own, send_marks, low, gradient, energy_out, low_out
 ):
     lane = lane_ids()[:TRIALS]
     sub = sub_ids()[:TRIALS]
@@ -356,7 +351,7 @@
             whole = moved if whole is None else jnp.where(wide == k, moved, whole)
         rows.append(whole)
     left = jnp.concatenate(split_three(jnp.concatenate(rows, axis=0)), axis=0)
-    found = by_marks(left, marks(send[...], own.shape[1]))
+    found = jnp.dot(left, send_marks[...], preferred_element_type=jnp.float32)
     height = 3 * SUBS
     found = found[:height] + found[height : 2 * height] + found[2 * height :]
     found = found + own[...]
@@ -447,16 +442,18 @@
         compiler_params=params,
         name="outgoing_nodes",
     )(*pinned(coords, direction, send_node))
-    came_at, slots, index, inverse, heavy, spots = pl.pallas_call(
+    came_at, slots, index, corners, inverse, heavy, spots, send_marks = pl.pallas_call(
         functools.partial(prepare_kernel, blocks),
-        in_specs=[hbm] * 4,
+        in_specs=[pl.BlockSpec(memory_space=pltpu.VMEM)] * 2 + [hbm] * 4,
         out_shape=(
             shaped((SUBS, LANES), i32),
             shaped(recv_slot.shape, i32),
             shaped((4, SUBS, elems // 2), i32),
+            shaped((12, SUBS, elems // 2), f32),
             shaped((9, SUBS, elems // 2), f32),
             shaped((SUBS, elems // 2), f32),
             shaped((2, 2 * elems, local), jnp.bfloat16),
+            shaped((LANES, owned), jnp.bfloat16),
         ),
         scratch_shapes=[
             pltpu.VMEM(connect.shape, i32),
@@ -467,7 +464,10 @@
         compiler_params=params,
         cost_estimate=pl.CostEstimate(flops=1000000, bytes_accessed=4000000, transcendentals=0),
         name="prepared_elements",
-    )(*pinned(recv_slot, connect, shape_inv, weight.reshape(elems // LANES, LANES)))
+    )(
+        table, sends,
+        *pinned(recv_slot, connect, shape_inv, weight.reshape(elems // LANES, LANES)),
+    )
     came = exchanged(outgoing, doms, subs)
     lows, jac = pl.pallas_call(
         functools.partial(det_kernel, blocks, exchanges(subs)),
@@ -475,10 +475,10 @@
             shaped((count, LANES), f32),
             shaped((9, SUBS, elems // 2), f32),
         ),
-        scratch_shapes=[pltpu.VMEM((SUBS, local), f32)],
+        scratch_shapes=[pltpu.VMEM((SUBS, LANES), f32)],
         compiler_params=params,
         name="jacobian_dets",
-    )(table, *came[::-1], index, inverse, came_at)
+    )(corners, *came[::-1], index, inverse, came_at)
     lows = lax.all_to_all(lows.reshape(count, 1, LANES), AXES, 0, 0).reshape(count, LANES)
     own, back, low = pl.pallas_call(
         functools.partial(grad_kernel, blocks, subs, doms),
@@ -500,7 +500,7 @@
         ),
         compiler_params=params,
         name="owner_sums",
-    )(back, own, sends, low)
+    )(back, own, send_marks, low)
     return gradient.transpose(1, 0, 2), energy.reshape(TRIALS), lowest.reshape(TRIALS)
 
 

time: 32.1 us -> 32 us (level)
  no operation moved by 1% of the time
where the time goes in v4:
time: 32 us; the launch traced here: 31.7 us
  blocking collectives  17.9 us (56%)
  starting transfers between devices  7.26 us (23%)
  Pallas kernels  4.86 us (15%)
  waiting for transfers between devices  1.03 us (3%)
  between operations  0.67 us (2%)
    all_to_all x1, blocking collectives, per_device(): back = lax.all_to_all(back, AXES, 0, 0)  9.08 us
    all_to_all x1, blocking collectives, per_device(): lax.all_to_all(lows.reshape(count, 1, LANES), AXES, 0, 0)  8.83 us
    ppermute x4, starting transfers between devices, exchanged(): lax.ppermute(tile, AXES, [(dom * subs + sub, partner(orders[sub][step], d...  7.26 us
    pallas_call x1, Pallas kernels, per_device(): pl.pallas_call(functools.partial(prepare_kernel, blocks), in_specs=[pl.Bl...  2.01 us
    ppermute x4, waiting for transfers between devices, exchanged(): lax.ppermute(tile, AXES, [(dom * subs + sub, partner(orders[sub][step], d...  1.03 us
    pallas_call x1, Pallas kernels, per_device(): pl.pallas_call(functools.partial(grad_kernel, blocks, subs, doms), out_sh...  0.86 us
    pallas_call x1, Pallas kernels, per_device(): pl.pallas_call(functools.partial(final_kernel, subs, doms, float(elems *...  0.82 us
    pallas_call x1, Pallas kernels, per_device(): pl.pallas_call(send_kernel, in_specs=[hbm] * 3, out_shape=(shaped((SUBS,...  0.81 us
  transfers between devices with their start and end apart: 4, of which 1 were waited for; matrix products, arithmetic and copies ran while one was open for 0% of the time, Pallas kernels for 6%

profile of v4, /device:TPU:0, one launch (start us, length us, event | category | flops | bytes accessed | tf_op | source)
XLA Modules:
  0.0 31.7 jit_solution(5024089255388139742)
XLA Ops:
  0.6 0.8 %outgoing_nodes.1 = (f32[8,128]{1,0:T(8,128)S(1)}, f32[8,256]{1,0:T(8,128)S(1)}, s32[1,128]{1,0:T(1,128)S(1)}) custom-call(f32[3,256]{1,0:T(4,128)} %coords.1, f32[3,256]{1,0:T(4,128)} %direction.1, s32[1,128]{1,0:T(1,128)} %send.1), custom_call_target="tpu_custom_call" | custom-call | tf_op jit(solution)/shard_map/outgoing_nodes/pallas_call | solution.py:429
  1.4 4.0 %collective-permute-start.3 = (f32[8,128]{1,0:T(8,128)S(1)}, f32[8,128]{1,0:T(8,128)S(1)}, u32[]{:S(2)}, u32[]{:S(2)}) collective-permute-start(f32[8,128]{1,0:T(8,128)S(1)} %get-tuple-element.25), channel_id=1, source_target_pairs={{0,24},{1,25},{2,26},{3,27},{4,28},{5,29},{6,30},{7,31},{8,16},{9,... | collective-permute-start | bytes 12296 | tf_op jit(solution)/shard_map/ppermute | solution.py:386
  5.4 2.8 %collective-permute-start.2 = (f32[8,128]{1,0:T(8,128)S(1)}, f32[8,128]{1,0:T(8,128)S(1)}, u32[]{:S(2)}, u32[]{:S(2)}) collective-permute-start(f32[8,128]{1,0:T(8,128)S(1)} %get-tuple-element.25), channel_id=1, source_target_pairs={{0,7},{1,2},{2,1},{3,4},{4,3},{5,6},{6,5},{7,0},{8,15},{9,10},{10,... | collective-permute-start | bytes 12296 | tf_op jit(solution)/shard_map/ppermute | solution.py:386
  8.2 0.5 %collective-permute-start.1 = (f32[8,128]{1,0:T(8,128)S(1)}, f32[8,128]{1,0:T(8,128)S(1)}, u32[]{:S(2)}, u32[]{:S(2)}) collective-permute-start(f32[8,128]{1,0:T(8,128)S(1)} %get-tuple-element.25), channel_id=1, source_target_pairs={{0,8},{1,9},{2,10},{3,11},{4,12},{5,13},{6,14},{7,15},{8,0},{9,1},... | collective-permute-start | bytes 12296 | tf_op jit(solution)/shard_map/ppermute | solution.py:386
  8.7 0.0 collective-permute-start
  8.7 2.0 %prepared_elements.1 = (s32[8,128]{1,0:T(8,128)S(1)}, s32[1,128]{1,0:T(1,128)S(1)}, s32[4,8,512]{2,1,0:T(8,128)S(1)}, f32[12,8,512]{2,1,0:T(8,128)S(1)}, f32[9,8...) custom-call(f32[8,256]{1,0:T(8,128)S(1)} %get-tuple-element.22.table, ...), custom_call_target="tpu_custom_call" | custom-call | flops 1000000 | bytes 4000000 | tf_op jit(solution)/shard_map/prepared_elements/pallas_call | solution.py:445
  10.7 0.0 collective-permute-done.3.came0
  10.7 0.0 collective-permute-done.2.came1
  10.8 1.0 %collective-permute-done.1.came2 = f32[8,128]{1,0:T(8,128)S(1)} collective-permute-done((f32[8,128]{1,0:T(8,128)S(1)}, f32[8,128]{1,0:T(8,128)S(1)}, u32[]{:S(2)}, u32[]{:S(2)}) %collective-permute-start.1) | collective-permute-done | bytes 4128 | tf_op jit(solution)/shard_map/ppermute | solution.py:386
  11.8 0.0 collective-permute-done.came3
  11.8 0.4 %jacobian_dets.1 = (f32[32,128]{1,0:T(8,128)S(1)}, f32[9,8,512]{2,1,0:T(8,128)S(1)}) custom-call(f32[12,8,512]{2,1,0:T(8,128)S(1)} %get-tuple-element.24.corner_in, f32[8,128]{1,0:T(8,128)S(1)} %collective-permute-done.came3, f32[8,128]{1,0:T(8,128)S(1)} %collective-permute-done.1.came2, f32[8,128]{1,0:T(8,128)S(1)} %collective-permute-done.2.came1, ...), custom_call_target="tpu_custom_call" | custom-call | tf_op jit(solution)/shard_map/jacobian_dets/pallas_call | solution.py:472
  12.1 8.8 %all_to_all.10 = f32[32,1,128]{2,1,0:T(1,128)S(1)} all-to-all(f32[32,1,128]{2,1,0:T(1,128)S(1)} %bitcast.9), channel_id=1, replica_groups=mesh['dom'=4,'sub'=8] {'dom','sub'}, dimensions={0} | all-to-all | bytes 32768 | tf_op jit(solution)/shard_map/all_to_all | solution.py:482
  21.0 0.9 %element_gradients.1 = (f32[24,256]{1,0:T(8,128)S(1)}, f32[32,4,128]{2,1,0:T(4,128)S(1)}, f32[1,128]{1,0:T(1,128)S(1)}) custom-call(f32[32,128]{1,0:T(8,128)S(1)} %bitcast.8, f32[9,8,512]{2,1,0:T(8,128)S(1)} %get-tuple-element.30.jac_in, f32[8,512]{1,0:T(8,128)S(1)} %get-tuple-element.31.weight, bf16[2,2048,384]{2,1,0:T(8,128)(2,1)S(1)} %get-tuple-element.32.spots, ...), custom_call_target="tpu_custom_call" | custom-call | tf_op jit(solution)/shard_map/element_gradients/pallas_call | solution.py:483
  21.8 9.1 %all_to_all.11.back = f32[32,4,128]{2,1,0:T(4,128)S(1)} all-to-all(f32[32,4,128]{2,1,0:T(4,128)S(1)} %get-tuple-element.34), channel_id=1, replica_groups=mesh['dom'=4,'sub'=8] {'dom','sub'}, dimensions={0} | all-to-all | bytes 131072 | tf_op jit(solution)/shard_map/all_to_all | solution.py:493
  30.9 0.8 %owner_sums.1 = (f32[3,4,256]{2,1,0:T(4,128)}, f32[1,4]{1,0:T(1,128)}, f32[1,4]{1,0:T(1,128)}) custom-call(f32[32,4,128]{2,1,0:T(4,128)S(1)} %all_to_all.11.back, f32[24,256]{1,0:T(8,128)S(1)} %get-tuple-element.35.own, bf16[128,256]{1,0:T(8,128)(2,1)S(1)} %get-tuple-element.36.send_marks, f32[1,128]{1,0:T(1,128)S(1)} %get-tuple-element.37.low), custom_call_target="tpu_custom_call" | custom-call | tf_op jit(solution)/shard_map/owner_sums/pallas_call | solution.py:494
Async XLA Ops:
  1.4 9.3 %collective-permute-start.3 = (f32[8,128]{1,0:T(8,128)S(1)}, f32[8,128]{1,0:T(8,128)S(1)}, u32[]{:S(2)}, u32[]{:S(2)}) collective-permute-start(f32[8,128]{1,0:T(8,128)S(1)} %get-tuple-element.25), channel_id=1, source_target_pairs={{0,24},{1,25},{2,26},{3,27},{4,28},{5,29},{6,30},{7,31},{8,16},{9,... | collective-permute-start | bytes 12296 | tf_op jit(solution)/shard_map/ppermute | solution.py:386
  5.4 5.3 %collective-permute-start.2 = (f32[8,128]{1,0:T(8,128)S(1)}, f32[8,128]{1,0:T(8,128)S(1)}, u32[]{:S(2)}, u32[]{:S(2)}) collective-permute-start(f32[8,128]{1,0:T(8,128)S(1)} %get-tuple-element.25), channel_id=1, source_target_pairs={{0,7},{1,2},{2,1},{3,4},{4,3},{5,6},{6,5},{7,0},{8,15},{9,10},{10,... | collective-permute-start | bytes 12296 | tf_op jit(solution)/shard_map/ppermute | solution.py:386
  8.2 3.6 %collective-permute-start.1 = (f32[8,128]{1,0:T(8,128)S(1)}, f32[8,128]{1,0:T(8,128)S(1)}, u32[]{:S(2)}, u32[]{:S(2)}) collective-permute-start(f32[8,128]{1,0:T(8,128)S(1)} %get-tuple-element.25), channel_id=1, source_target_pairs={{0,8},{1,9},{2,10},{3,11},{4,12},{5,13},{6,14},{7,15},{8,0},{9,1},... | collective-permute-start | bytes 12296 | tf_op jit(solution)/shard_map/ppermute | solution.py:386
  8.7 3.1 %collective-permute-start = (f32[8,128]{1,0:T(8,128)S(1)}, f32[8,128]{1,0:T(8,128)S(1)}, u32[]{:S(2)}, u32[]{:S(2)}) collective-permute-start(f32[8,128]{1,0:T(8,128)S(1)} %get-tuple-element.25), channel_id=1, source_target_pairs={{0,1},{1,0},{2,3},{3,2},{4,5},{5,4},{6,7},{7,6},{8,9},{9,8},{10,11... | collective-permute-start | bytes 12296 | tf_op jit(solution)/shard_map/ppermute | solution.py:386

commit v5 on v4

--- a/solution.py
+++ b/solution.py
@@ -10,6 +10,7 @@
 TRIALS = 4
 AXES = ("dom", "sub")
 LANES = 128
+SHARE = 32
 SUBS = 8
 
 
@@ -88,13 +89,21 @@
 
 
 def send_kernel(
-    coords, direction, send, out, table, send_out, coords_in, direction_in, arrived
+    coords, direction, send, slots, connect,
+    out, table, send_out, slots_out, connect_out, coords_in, direction_in, arrived,
 ):
     copies = fetch(
-        ((coords, coords_in), (direction, direction_in), (send, send_out)), arrived
+        (
+            (coords, coords_in),
+            (direction, direction_in),
+            (send, send_out),
+            (slots, slots_out),
+            (connect, connect_out),
+        ),
+        arrived,
     )
     table[...] = jnp.zeros_like(table)
-    for copy in copies:
+    for copy in copies[:3]:
         copy.wait()
     table[0:3, :] = coords_in[...]
     table[3:6, :] = direction_in[...]
@@ -103,67 +112,60 @@
     first = picked(table[:, :LANES], low)
     second = picked(table[:, LANES:], low)
     out[...] = jnp.where(index < LANES, first, second)
+    for copy in copies[3:]:
+        copy.wait()
 
 
 def prepare_kernel(
-    blocks, table, sends, slots, connect, inverse, weight,
-    came_out, slots_out, index_out, corner_out, inverse_out, weight_out, marks_out,
-    send_marks_out, connect_in, inverse_in, weight_in, arrived,
+    blocks, table, sends, slots_in, connect_in, inverse, weight,
+    index_out, corner_out, inverse_out, weight_out, marks_out, send_marks_out,
+    inverse_in, weight_in, arrived,
 ):
-    copies = fetch(
-        (
-            (connect, connect_in),
-            (slots, slots_out),
-            (weight, weight_in),
-            (inverse, inverse_in),
-        ),
-        arrived,
-    )
+    copies = fetch(((weight, weight_in), (inverse, inverse_in)), arrived)
     steps = step_lengths()
     firsts, seconds = trial_places(table, 0, steps), trial_places(table, 1, steps)
-    columns = jnp.transpose(spread(sends[...]))
-    send_marks_out[...] = column_marks(columns[:, :1], send_marks_out.shape[1])
-    copies[0].wait()
-    width = blocks * LANES
-    for corner in range(4):
-        for block in range(blocks):
-            cut = slice(block * LANES, (block + 1) * LANES)
+    owned = table.shape[1]
+    nodes = marks_out.shape[2]
+    order = marks(slots_in[...], LANES)
+    entry = lax.broadcasted_iota(jnp.int32, (16, LANES), 1).astype(jnp.bfloat16)
+    came_at = by_marks(entry, order)[:SUBS].astype(jnp.int32)
+
+    def renumbered(given):
+        moved = owned + picked(came_at, given & (LANES - 1))
+        return jnp.where(given < owned, given, moved)
+
+    for block in range(blocks):
+        cut = slice(block * LANES, (block + 1) * LANES)
+        for corner in range(4):
             index = halves(connect_in, corner, block, blocks)
-            index_out[corner, :, cut] = index
             low = index & (LANES - 1)
             for comp in range(3):
                 corner_out[3 * corner + comp, :, cut] = jnp.where(
                     index < LANES, picked(firsts[comp], low), picked(seconds[comp], low)
                 )
-    nodes = marks_out.shape[2]
-    for half in range(2):
-        for block in range(blocks):
-            start = half * width + block * LANES
-            columns = jnp.transpose(
-                jnp.concatenate([connect_in[:, start : start + LANES]] * 2, axis=0)
+            index_out[corner, :, cut] = renumbered(index)
+    columns = jnp.transpose(spread(sends[...]))
+    send_marks_out[...] = column_marks(columns[:, :1], send_marks_out.shape[1])
+    for block in range(2 * blocks):
+        given = connect_in[:, block * LANES : (block + 1) * LANES]
+        columns = jnp.transpose(renumbered(jnp.concatenate([given, given], axis=0)))
+        half, place = block // blocks, block % blocks
+        for corner in range(4):
+            row = (4 * place + corner) * LANES
+            marks_out[half, row : row + LANES, :] = column_marks(
+                columns[:, corner : corner + 1], nodes
             )
-            for corner in range(4):
-                row = (4 * block + corner) * LANES
-                marks_out[half, row : row + LANES, :] = column_marks(
-                    columns[:, corner : corner + 1], nodes
-                )
-    copies[1].wait()
-    order = marks(slots_out[...], LANES)
-    entry = lax.broadcasted_iota(jnp.int32, (16, LANES), 1).astype(jnp.bfloat16)
-    came_out[...] = by_marks(entry, order)[:SUBS].astype(jnp.int32)
-    copies[2].wait()
+    for copy in copies:
+        copy.wait()
     for block in range(blocks):
-        weight_out[:, block * LANES : (block + 1) * LANES] = jnp.where(
+        cut = slice(block * LANES, (block + 1) * LANES)
+        weight_out[:, cut] = jnp.where(
             sub_ids() < TRIALS,
             spread(weight_in[block : block + 1, :]),
             spread(weight_in[blocks + block : blocks + block + 1, :]),
         )
-    copies[3].wait()
-    for row in range(9):
-        for block in range(blocks):
-            inverse_out[row, :, block * LANES : (block + 1) * LANES] = halves(
-                inverse_in, row, block, blocks
-            )
+        for row in range(9):
+            inverse_out[row, :, cut] = halves(inverse_in, row, block, blocks)
 
 
 def cofactor(m):
@@ -187,24 +189,18 @@
 
 
 def det_kernel(
-    blocks, orders, corner_in, came3, came2, came1, came0, connect, inverse, came_at,
+    blocks, owned, corner_in, near_sub, near_dom, far_sub, far_dom, connect, inverse,
     low_out, jac_out, table,
 ):
     lane = lane_ids()
-    group = lane // 32
-    came = (came0, came1, came2, came3)
-    near_dom, far_dom, near_sub, far_sub = (
-        tile_of(kind, orders, came) for kind in ("near_dom", "far_dom", "near_sub", "far_sub")
-    )
+    group = lane // SHARE
     from_before = group & 1
-    arrived = jnp.where(
+    table[...] = jnp.where(
         group < 2,
-        jnp.where(from_before != (lax.axis_index("dom") & 1), near_dom, far_dom),
-        jnp.where(from_before != (lax.axis_index("sub") & 1), near_sub, far_sub),
-    )
-    table[...] = picked(arrived, came_at[...])
+        jnp.where(from_before != (lax.axis_index("dom") & 1), near_dom[...], far_dom[...]),
+        jnp.where(from_before != (lax.axis_index("sub") & 1), near_sub[...], far_sub[...]),
+    )
     ghosts = trial_places(table, 0, step_lengths())
-    owned = 2 * LANES
     lowest = None
     for block in range(blocks):
         cut = slice(block * LANES, (block + 1) * LANES)
@@ -251,7 +247,7 @@
 
 
 def grad_kernel(
-    blocks, sub_count, dom_count, lows, jac_in, weight, spots, inverse, slots,
+    blocks, sub_count, dom_count, lows, jac_in, weight, spots, inverse,
     own_out, back_out, low_out,
 ):
     lane, sub = lane_ids(), sub_ids()
@@ -305,7 +301,7 @@
         mixed = jnp.where(upper, sums[0][cut], sums[1][cut])
         both = mixed + pltpu.roll(mixed, TRIALS, 0)
         own_out[cut, :] = both[:, : local - LANES]
-        ghosts.append(picked(both[:, local - LANES :], spread(slots[...])))
+        ghosts.append(both[:, local - LANES :])
     energy = spread_lanes(jnp.sum(energy, axis=1, keepdims=True))
     energy = energy + pltpu.roll(energy, TRIALS, 0)
     back_out[...] = jnp.broadcast_to(energy[None, :TRIALS], back_out.shape)
@@ -316,11 +312,11 @@
         dom * sub_count + lax.rem(part + sub_count - 1, sub_count),
         dom * sub_count + lax.rem(part + 1, sub_count),
     )
-    group = lane // 32
+    group = lane // SHARE
     for k in range(4):
         tile = energy
         for comp in range(3):
-            turned = (32 * (comp - k)) % LANES
+            turned = (SHARE * (comp - k)) % LANES
             moved = pltpu.roll(ghosts[comp], turned, 1) if turned else ghosts[comp]
             tile = jnp.where(group == comp, moved, tile)
         back_out[targets[k]] = tile[:TRIALS]
@@ -331,7 +327,7 @@
 ):
     lane = lane_ids()[:TRIALS]
     sub = sub_ids()[:TRIALS]
-    group = lane // 32
+    group = lane // SHARE
     dom, part = lax.axis_index("dom"), lax.axis_index("sub")
     sources = (
         lax.rem(dom + 1, dom_count) * sub_count + part,
@@ -341,12 +337,12 @@
     )
     came = [back[sources[k]] for k in range(4)]
     came = [jnp.concatenate([tile, tile], axis=0) for tile in came]
-    wide = lane_ids() // 32
+    wide = lane_ids() // SHARE
     rows = []
     for comp in range(3):
         whole = None
         for k in range(4):
-            turned = (32 * (k - comp)) % LANES
+            turned = (SHARE * (k - comp)) % LANES
             moved = pltpu.roll(came[k], turned, 1) if turned else came[k]
             whole = moved if whole is None else jnp.where(wide == k, moved, whole)
         rows.append(whole)
@@ -364,51 +360,13 @@
     low_out[...] = low[:, :TRIALS]
 
 
-def partner(kind, doms, subs, dom, sub):
-    if kind == "near_dom":
-        return (dom ^ 1) * subs + sub
-    if kind == "far_dom":
-        return ((dom + 1 if dom % 2 else dom - 1) % doms) * subs + sub
-    if kind == "near_sub":
-        return dom * subs + (sub ^ 1)
-    return dom * subs + (sub + 1 if sub % 2 else sub - 1) % subs
-
-
-def exchanges(subs):
-    usual = ("far_dom", "far_sub", "near_dom", "near_sub")
-    last = ("near_sub", "far_sub", "far_dom", "near_dom")
-    return [last if sub >= subs else usual for sub in range(subs)]
-
-
-def exchanged(tile, doms, subs):
-    orders = exchanges(subs)
-    return [
-        lax.ppermute(
-            tile,
-            AXES,
-            [
-                (dom * subs + sub, partner(orders[sub][step], doms, subs, dom, sub))
-                for dom in range(doms)
-                for sub in range(subs)
-            ],
-        )
-        for step in range(4)
-    ]
-
-
-def tile_of(kind, orders, came):
-    sub = lax.axis_index("sub")
-    tile = None
-    for step in range(4):
-        places = [place for place, order in enumerate(orders) if order[step] == kind]
-        if not places:
-            continue
-        if tile is None:
-            tile = came[step][...]
-            continue
-        here = functools.reduce(jnp.logical_or, [sub == place for place in places])
-        tile = jnp.where(here, came[step][...], tile)
-    return tile
+def exchanged(tile, axis):
+    count = lax.axis_size(axis)
+    near = lax.ppermute(tile, axis, [(i, i ^ 1) for i in range(count)])
+    far = lax.ppermute(
+        tile, axis, [(i, (i + 1 if i % 2 else i - 1) % count) for i in range(count)]
+    )
+    return near, far
 
 
 def per_device(coords, direction, connect, shape_inv, weight, send_node, recv_slot):
@@ -426,28 +384,28 @@
     def pinned(*arrays):
         return [pltpu.with_memory_space_constraint(x, pltpu.HBM) for x in arrays]
 
-    outgoing, table, sends = pl.pallas_call(
+    outgoing, table, sends, slots, connect = pl.pallas_call(
         send_kernel,
-        in_specs=[hbm] * 3,
+        in_specs=[hbm] * 5,
         out_shape=(
             shaped((SUBS, LANES), f32),
             shaped((SUBS, owned), f32),
             shaped(send_node.shape, i32),
+            shaped(recv_slot.shape, i32),
+            shaped(connect.shape, i32),
         ),
         scratch_shapes=[
             pltpu.VMEM(coords.shape, f32),
             pltpu.VMEM(direction.shape, f32),
-            pltpu.SemaphoreType.DMA((3,)),
+            pltpu.SemaphoreType.DMA((5,)),
         ],
         compiler_params=params,
         name="outgoing_nodes",
-    )(*pinned(coords, direction, send_node))
-    came_at, slots, index, corners, inverse, heavy, spots, send_marks = pl.pallas_call(
+    )(*pinned(coords, direction, send_node, recv_slot, connect))
+    index, corners, inverse, heavy, spots, send_marks = pl.pallas_call(
         functools.partial(prepare_kernel, blocks),
-        in_specs=[pl.BlockSpec(memory_space=pltpu.VMEM)] * 2 + [hbm] * 4,
+        in_specs=[pl.BlockSpec(memory_space=pltpu.VMEM)] * 4 + [hbm] * 2,
         out_shape=(
-            shaped((SUBS, LANES), i32),
-            shaped(recv_slot.shape, i32),
             shaped((4, SUBS, elems // 2), i32),
             shaped((12, SUBS, elems // 2), f32),
             shaped((9, SUBS, elems // 2), f32),
@@ -456,21 +414,21 @@
             shaped((LANES, owned), jnp.bfloat16),
         ),
         scratch_shapes=[
-            pltpu.VMEM(connect.shape, i32),
             pltpu.VMEM(shape_inv.shape, f32),
             pltpu.VMEM((elems // LANES, LANES), f32),
-            pltpu.SemaphoreType.DMA((4,)),
+            pltpu.SemaphoreType.DMA((2,)),
         ],
         compiler_params=params,
         cost_estimate=pl.CostEstimate(flops=1000000, bytes_accessed=4000000, transcendentals=0),
         name="prepared_elements",
     )(
-        table, sends,
-        *pinned(recv_slot, connect, shape_inv, weight.reshape(elems // LANES, LANES)),
-    )
-    came = exchanged(outgoing, doms, subs)
+        table, sends, slots, connect,
+        *pinned(shape_inv, weight.reshape(elems // LANES, LANES)),
+    )
+    near_dom, far_dom = exchanged(outgoing, "dom")
+    near_sub, far_sub = exchanged(outgoing, "sub")
     lows, jac = pl.pallas_call(
-        functools.partial(det_kernel, blocks, exchanges(subs)),
+        functools.partial(det_kernel, blocks, owned),
         out_shape=(
             shaped((count, LANES), f32),
             shaped((9, SUBS, elems // 2), f32),
@@ -478,7 +436,7 @@
         scratch_shapes=[pltpu.VMEM((SUBS, LANES), f32)],
         compiler_params=params,
         name="jacobian_dets",
-    )(corners, *came[::-1], index, inverse, came_at)
+    )(corners, near_sub, near_dom, far_sub, far_dom, index, inverse)
     lows = lax.all_to_all(lows.reshape(count, 1, LANES), AXES, 0, 0).reshape(count, LANES)
     own, back, low = pl.pallas_call(
         functools.partial(grad_kernel, blocks, subs, doms),
@@ -489,7 +447,7 @@
         ),
         compiler_params=params,
         name="element_gradients",
-    )(lows, jac, heavy, spots, inverse, slots)
+    )(lows, jac, heavy, spots, inverse)
     back = lax.all_to_all(back, AXES, 0, 0)
     gradient, energy, lowest = pl.pallas_call(
         functools.partial(final_kernel, subs, doms, float(elems * count)),

time: 32 us -> 31.9 us (level)
  Pallas kernels: 4.86 us -> 4.47 us
where the time goes in v5:
time: 31.9 us; the launch traced here: 31.6 us
  blocking collectives  17.9 us (56%)
  starting transfers between devices  7.26 us (23%)
  Pallas kernels  4.47 us (14%)
  waiting for transfers between devices  1.28 us (4%)
  between operations  0.67 us (2%)
    all_to_all x1, blocking collectives, per_device(): back = lax.all_to_all(back, AXES, 0, 0)  9.08 us
    all_to_all x1, blocking collectives, per_device(): lax.all_to_all(lows.reshape(count, 1, LANES), AXES, 0, 0)  8.83 us
    ppermute x2, starting transfers between devices, exchanged(): lax.ppermute(tile, axis, [(i, (i + 1 if i % 2 else i - 1) % count) for i...  6.72 us
    pallas_call x1, Pallas kernels, per_device(): pl.pallas_call(functools.partial(prepare_kernel, blocks), in_specs=[pl.Bl...  1.76 us
    ppermute x2, waiting for transfers between devices, exchanged(): near = lax.ppermute(tile, axis, [(i, i ^ 1) for i in range(count)])  1.28 us
    pallas_call x1, Pallas kernels, per_device(): pl.pallas_call(send_kernel, in_specs=[hbm] * 5, out_shape=(shaped((SUBS,...  0.83 us
    pallas_call x1, Pallas kernels, per_device(): pl.pallas_call(functools.partial(final_kernel, subs, doms, float(elems *...  0.82 us
    pallas_call x1, Pallas kernels, per_device(): pl.pallas_call(functools.partial(grad_kernel, blocks, subs, doms), out_sh...  0.77 us
  transfers between devices with their start and end apart: 4, of which 1 were waited for; matrix products, arithmetic and copies ran while one was open for 0% of the time, Pallas kernels for 6%

profile of v5, /device:TPU:0, one launch (start us, length us, event | category | flops | bytes accessed | tf_op | source)
XLA Modules:
  0.0 31.6 jit_solution(16905229645231755123)
XLA Ops:
  0.6 0.8 %outgoing_nodes.1 = (f32[8,128]{1,0:T(8,128)S(1)}, f32[8,256]{1,0:T(8,128)S(1)}, s32[1,128]{1,0:T(1,128)S(1)}, s32[1,128]{1,0:T(1,128)S(1)}, s32[4,1024]{1,0:T(4,128)S(1)}) custom-call(f32[3,256]{1,0:T(4,128)} %coords.1, f32[3,256]{1,0:T(4,128)} %direction.1, s32[1,128]{1,0:T(1,128)} %send.1, s32[1,128]{1,0:T(1,128)} %slots.1, s32[4,1024]{1,0:T(4,128)} %connect.1), custom_call_target="tpu_custom_call" | custom-call | tf_op jit(solution)/shard_map/outgoing_nodes/pallas_call | solution.py:387
  1.5 4.0 %collective-permute-start.3 = (f32[8,128]{1,0:T(8,128)S(1)}, f32[8,128]{1,0:T(8,128)S(1)}, u32[]{:S(2)}, u32[]{:S(2)}) collective-permute-start(f32[8,128]{1,0:T(8,128)S(1)} %get-tuple-element.27), channel_id=1, source_target_pairs={{0,24},{8,16},{16,8},{24,0},{1,25},{9,17},{17,9},{25,1},{2,26},{10... | collective-permute-start | bytes 12296 | tf_op jit(solution)/shard_map/ppermute | solution.py:366
  5.4 2.8 %collective-permute-start.2 = (f32[8,128]{1,0:T(8,128)S(1)}, f32[8,128]{1,0:T(8,128)S(1)}, u32[]{:S(2)}, u32[]{:S(2)}) collective-permute-start(f32[8,128]{1,0:T(8,128)S(1)} %get-tuple-element.27), channel_id=1, source_target_pairs={{0,7},{1,2},{2,1},{3,4},{4,3},{5,6},{6,5},{7,0},{8,15},{9,10},{10,... | collective-permute-start | bytes 12296 | tf_op jit(solution)/shard_map/ppermute | solution.py:366
  8.2 0.5 %collective-permute-start.1 = (f32[8,128]{1,0:T(8,128)S(1)}, f32[8,128]{1,0:T(8,128)S(1)}, u32[]{:S(2)}, u32[]{:S(2)}) collective-permute-start(f32[8,128]{1,0:T(8,128)S(1)} %get-tuple-element.27), channel_id=1, source_target_pairs={{0,8},{8,0},{16,24},{24,16},{1,9},{9,1},{17,25},{25,17},{2,10},{10... | collective-permute-start | bytes 12296 | tf_op jit(solution)/shard_map/ppermute | solution.py:365
  8.7 0.0 collective-permute-start
  8.7 1.8 %prepared_elements.1 = (s32[4,8,512]{2,1,0:T(8,128)S(1)}, f32[12,8,512]{2,1,0:T(8,128)S(1)}, f32[9,8,512]{2,1,0:T(8,128)S(1)}, f32[8,512]{1,0:T(8,128)S(1)}, bf1...) custom-call(f32[8,256]{1,0:T(8,128)S(1)} %get-tuple-element.22.table, s32[1,128]{1,0:T(1,128)S(1)} %get-tuple-element.23.sends, ...), custom_call_target="tpu_custom_call" | custom-call | flops 1000000 | bytes 4000000 | tf_op jit(solution)/shard_map/prepared_elements/pallas_call | solution.py:405
  10.5 0.0 collective-permute-done.3.far_dom
  10.5 0.0 collective-permute-done.2.far_sub
  10.5 1.3 %collective-permute-done.1.near_dom = f32[8,128]{1,0:T(8,128)S(1)} collective-permute-done((f32[8,128]{1,0:T(8,128)S(1)}, f32[8,128]{1,0:T(8,128)S(1)}, u32[]{:S(2)}, u32[]{:S(2)}) %collective-permute-start.1) | collective-permute-done | bytes 4128 | tf_op jit(solution)/shard_map/ppermute | solution.py:365
  11.8 0.0 collective-permute-done.near_sub
  11.8 0.3 jacobian_dets.1
  12.1 8.8 %all_to_all.10 = f32[32,1,128]{2,1,0:T(1,128)S(1)} all-to-all(f32[32,1,128]{2,1,0:T(1,128)S(1)} %bitcast.9), channel_id=1, replica_groups=mesh['dom'=4,'sub'=8] {'dom','sub'}, dimensions={0} | all-to-all | bytes 32768 | tf_op jit(solution)/shard_map/all_to_all | solution.py:440
  20.9 0.8 %element_gradients.1 = (f32[24,256]{1,0:T(8,128)S(1)}, f32[32,4,128]{2,1,0:T(4,128)S(1)}, f32[1,128]{1,0:T(1,128)S(1)}) custom-call(f32[32,128]{1,0:T(8,128)S(1)} %bitcast.8, f32[9,8,512]{2,1,0:T(8,128)S(1)} %get-tuple-element.31.jac_in, f32[8,512]{1,0:T(8,128)S(1)} %get-tuple-element.32.weight, bf16[2,2048,384]{2,1,0:T(8,128)(2,1)S(1)} %get-tuple-element.33.spots, ...), custom_call_target="tpu_custom_call" | custom-call | tf_op jit(solution)/shard_map/element_gradients/pallas_call | solution.py:441
  21.7 9.1 %all_to_all.11.back = f32[32,4,128]{2,1,0:T(4,128)S(1)} all-to-all(f32[32,4,128]{2,1,0:T(4,128)S(1)} %get-tuple-element.34), channel_id=1, replica_groups=mesh['dom'=4,'sub'=8] {'dom','sub'}, dimensions={0} | all-to-all | bytes 131072 | tf_op jit(solution)/shard_map/all_to_all | solution.py:451
  30.8 0.8 %owner_sums.1 = (f32[3,4,256]{2,1,0:T(4,128)}, f32[1,4]{1,0:T(1,128)}, f32[1,4]{1,0:T(1,128)}) custom-call(f32[32,4,128]{2,1,0:T(4,128)S(1)} %all_to_all.11.back, f32[24,256]{1,0:T(8,128)S(1)} %get-tuple-element.35.own, bf16[128,256]{1,0:T(8,128)(2,1)S(1)} %get-tuple-element.36.send_marks, f32[1,128]{1,0:T(1,128)S(1)} %get-tuple-element.37.low), custom_call_target="tpu_custom_call" | custom-call | tf_op jit(solution)/shard_map/owner_sums/pallas_call | solution.py:452
Async XLA Ops:
  1.5 9.0 %collective-permute-start.3 = (f32[8,128]{1,0:T(8,128)S(1)}, f32[8,128]{1,0:T(8,128)S(1)}, u32[]{:S(2)}, u32[]{:S(2)}) collective-permute-start(f32[8,128]{1,0:T(8,128)S(1)} %get-tuple-element.27), channel_id=1, source_target_pairs={{0,24},{8,16},{16,8},{24,0},{1,25},{9,17},{17,9},{25,1},{2,26},{10... | collective-permute-start | bytes 12296 | tf_op jit(solution)/shard_map/ppermute | solution.py:366
  5.4 5.1 %collective-permute-start.2 = (f32[8,128]{1,0:T(8,128)S(1)}, f32[8,128]{1,0:T(8,128)S(1)}, u32[]{:S(2)}, u32[]{:S(2)}) collective-permute-start(f32[8,128]{1,0:T(8,128)S(1)} %get-tuple-element.27), channel_id=1, source_target_pairs={{0,7},{1,2},{2,1},{3,4},{4,3},{5,6},{6,5},{7,0},{8,15},{9,10},{10,... | collective-permute-start | bytes 12296 | tf_op jit(solution)/shard_map/ppermute | solution.py:366
  8.2 3.6 %collective-permute-start.1 = (f32[8,128]{1,0:T(8,128)S(1)}, f32[8,128]{1,0:T(8,128)S(1)}, u32[]{:S(2)}, u32[]{:S(2)}) collective-permute-start(f32[8,128]{1,0:T(8,128)S(1)} %get-tuple-element.27), channel_id=1, source_target_pairs={{0,8},{8,0},{16,24},{24,16},{1,9},{9,1},{17,25},{25,17},{2,10},{10... | collective-permute-start | bytes 12296 | tf_op jit(solution)/shard_map/ppermute | solution.py:365
  8.7 3.1 %collective-permute-start = (f32[8,128]{1,0:T(8,128)S(1)}, f32[8,128]{1,0:T(8,128)S(1)}, u32[]{:S(2)}, u32[]{:S(2)}) collective-permute-start(f32[8,128]{1,0:T(8,128)S(1)} %get-tuple-element.27), channel_id=1, source_target_pairs={{0,1},{1,0},{2,3},{3,2},{4,5},{5,4},{6,7},{7,6},{8,9},{9,8},{10,11... | collective-permute-start | bytes 12296 | tf_op jit(solution)/shard_map/ppermute | solution.py:365

commit v6 on v5

--- a/solution.py
+++ b/solution.py
@@ -189,16 +189,20 @@
 
 
 def det_kernel(
-    blocks, owned, corner_in, near_sub, near_dom, far_sub, far_dom, connect, inverse,
+    blocks, owned, orders, corner_in, came3, came2, came1, came0, connect, inverse,
     low_out, jac_out, table,
 ):
+    came = (came0, came1, came2, came3)
+    near_dom, far_dom, near_sub, far_sub = (
+        tile_of(kind, orders, came) for kind in ("near_dom", "far_dom", "near_sub", "far_sub")
+    )
     lane = lane_ids()
     group = lane // SHARE
     from_before = group & 1
     table[...] = jnp.where(
         group < 2,
-        jnp.where(from_before != (lax.axis_index("dom") & 1), near_dom[...], far_dom[...]),
-        jnp.where(from_before != (lax.axis_index("sub") & 1), near_sub[...], far_sub[...]),
+        jnp.where(from_before != (lax.axis_index("dom") & 1), near_dom, far_dom),
+        jnp.where(from_before != (lax.axis_index("sub") & 1), near_sub, far_sub),
     )
     ghosts = trial_places(table, 0, step_lengths())
     lowest = None
@@ -360,13 +364,59 @@
     low_out[...] = low[:, :TRIALS]
 
 
-def exchanged(tile, axis):
-    count = lax.axis_size(axis)
-    near = lax.ppermute(tile, axis, [(i, i ^ 1) for i in range(count)])
-    far = lax.ppermute(
-        tile, axis, [(i, (i + 1 if i % 2 else i - 1) % count) for i in range(count)]
-    )
-    return near, far
+def partner(kind, doms, subs, dom, sub):
+    if kind == "near_dom":
+        return (dom ^ 1) * subs + sub
+    if kind == "far_dom":
+        return ((dom + 1 if dom % 2 else dom - 1) % doms) * subs + sub
+    if kind == "near_sub":
+        return dom * subs + (sub ^ 1)
+    return dom * subs + (sub + 1 if sub % 2 else sub - 1) % subs
+
+
+KINDS = {"f": "far_dom", "n": "near_dom", "s": "far_sub", "c": "near_sub"}
+FIRST_ORDERS = ("fsnc", "nsfc", "csnf", "csfn")
+LAST_ORDERS = ("nsfc", "fsnc", "fscn", "nscf")
+
+
+def exchanges(subs):
+    ends = len(FIRST_ORDERS) + len(LAST_ORDERS)
+    if subs < ends:
+        orders = ("fsnc",) * subs
+    else:
+        orders = FIRST_ORDERS + ("fsnc",) * (subs - ends) + LAST_ORDERS
+    return [tuple(KINDS[letter] for letter in order) for order in orders]
+
+
+def exchanged(tile, doms, subs):
+    orders = exchanges(subs)
+    return [
+        lax.ppermute(
+            tile,
+            AXES,
+            [
+                (dom * subs + sub, partner(orders[sub][step], doms, subs, dom, sub))
+                for dom in range(doms)
+                for sub in range(subs)
+            ],
+        )
+        for step in range(4)
+    ]
+
+
+def tile_of(kind, orders, came):
+    sub = lax.axis_index("sub")
+    tile = None
+    for step in range(4):
+        places = [place for place, order in enumerate(orders) if order[step] == kind]
+        if not places:
+            continue
+        if tile is None:
+            tile = came[step][...]
+            continue
+        here = functools.reduce(jnp.logical_or, [sub == place for place in places])
+        tile = jnp.where(here, came[step][...], tile)
+    return tile
 
 
 def per_device(coords, direction, connect, shape_inv, weight, send_node, recv_slot):
@@ -425,10 +475,9 @@
         table, sends, slots, connect,
         *pinned(shape_inv, weight.reshape(elems // LANES, LANES)),
     )
-    near_dom, far_dom = exchanged(outgoing, "dom")
-    near_sub, far_sub = exchanged(outgoing, "sub")
+    came = exchanged(outgoing, doms, subs)
     lows, jac = pl.pallas_call(
-        functools.partial(det_kernel, blocks, owned),
+        functools.partial(det_kernel, blocks, owned, exchanges(subs)),
         out_shape=(
             shaped((count, LANES), f32),
             shaped((9, SUBS, elems // 2), f32),
@@ -436,7 +485,7 @@
         scratch_shapes=[pltpu.VMEM((SUBS, LANES), f32)],
         compiler_params=params,
         name="jacobian_dets",
-    )(corners, near_sub, near_dom, far_sub, far_dom, index, inverse)
+    )(corners, *came[::-1], index, inverse)
     lows = lax.all_to_all(lows.reshape(count, 1, LANES), AXES, 0, 0).reshape(count, LANES)
     own, back, low = pl.pallas_call(
         functools.partial(grad_kernel, blocks, subs, doms),

time: 31.9 us -> 31.6 us (level)
  starting transfers between devices: 7.26 us -> 6.3 us
  blocking collectives: 17.9 us -> 18.6 us
    ppermute x4, starting transfers between devices: 7.26 us -> 6.3 us  [exchanged(): lax.ppermute(tile, AXES, [(dom * subs + sub, partner(orders[sub][step], d...]
    all_to_all x1, blocking collectives: 8.83 us -> 9.51 us  [per_device(): lax.all_to_all(lows.reshape(count, 1, LANES), AXES, 0, 0)]
  transfers between devices with their start and end apart: 4 -> 4, of which waited for: 1 -> 2; matrix products, arithmetic and copies ran while one was open for 0% -> 0% of each run, Pallas kernels for 6% -> 6%
where the time goes in v6:
time: 31.6 us; the launch traced here: 31.3 us
  blocking collectives  18.6 us (59%)
  starting transfers between devices  6.3 us (20%)
  Pallas kernels  4.48 us (14%)
  waiting for transfers between devices  1.29 us (4%)
  between operations  0.66 us (2%)
    all_to_all x1, blocking collectives, per_device(): lax.all_to_all(lows.reshape(count, 1, LANES), AXES, 0, 0)  9.51 us
    all_to_all x1, blocking collectives, per_device(): back = lax.all_to_all(back, AXES, 0, 0)  9.08 us
    ppermute x4, starting transfers between devices, exchanged(): lax.ppermute(tile, AXES, [(dom * subs + sub, partner(orders[sub][step], d...  6.3 us
    pallas_call x1, Pallas kernels, per_device(): pl.pallas_call(functools.partial(prepare_kernel, blocks), in_specs=[pl.Bl...  1.76 us
    ppermute x4, waiting for transfers between devices, exchanged(): lax.ppermute(tile, AXES, [(dom * subs + sub, partner(orders[sub][step], d...  1.29 us
    pallas_call x1, Pallas kernels, per_device(): pl.pallas_call(send_kernel, in_specs=[hbm] * 5, out_shape=(shaped((SUBS,...  0.83 us
    pallas_call x1, Pallas kernels, per_device(): pl.pallas_call(functools.partial(final_kernel, subs, doms, float(elems *...  0.82 us
    pallas_call x1, Pallas kernels, per_device(): pl.pallas_call(functools.partial(grad_kernel, blocks, subs, doms), out_sh...  0.77 us
  transfers between devices with their start and end apart: 4, of which 2 were waited for; matrix products, arithmetic and copies ran while one was open for 0% of the time, Pallas kernels for 6%

profile of v6, /device:TPU:0, one launch (start us, length us, event | category | flops | bytes accessed | tf_op | source)
XLA Modules:
  0.0 31.3 jit_solution(15244940445673346527)
XLA Ops:
  0.6 0.8 %outgoing_nodes.1 = (f32[8,128]{1,0:T(8,128)S(1)}, f32[8,256]{1,0:T(8,128)S(1)}, s32[1,128]{1,0:T(1,128)S(1)}, s32[1,128]{1,0:T(1,128)S(1)}, s32[4,1024]{1,0:T(4,128)S(1)}) custom-call(f32[3,256]{1,0:T(4,128)} %coords.1, f32[3,256]{1,0:T(4,128)} %direction.1, s32[1,128]{1,0:T(1,128)} %send.1, s32[1,128]{1,0:T(1,128)} %slots.1, s32[4,1024]{1,0:T(4,128)} %connect.1), custom_call_target="tpu_custom_call" | custom-call | tf_op jit(solution)/shard_map/outgoing_nodes/pallas_call | solution.py:437
  1.5 4.0 %collective-permute-start.3 = (f32[8,128]{1,0:T(8,128)S(1)}, f32[8,128]{1,0:T(8,128)S(1)}, u32[]{:S(2)}, u32[]{:S(2)}) collective-permute-start(f32[8,128]{1,0:T(8,128)S(1)} %get-tuple-element.27), channel_id=1, source_target_pairs={{0,24},{1,9},{2,3},{3,2},{4,12},{5,29},{6,30},{7,15},{8,16},{9,1},... | collective-permute-start | bytes 12296 | tf_op jit(solution)/shard_map/ppermute | solution.py:394
  5.4 1.8 %collective-permute-start.2 = (f32[8,128]{1,0:T(8,128)S(1)}, f32[8,128]{1,0:T(8,128)S(1)}, u32[]{:S(2)}, u32[]{:S(2)}) collective-permute-start(f32[8,128]{1,0:T(8,128)S(1)} %get-tuple-element.27), channel_id=1, source_target_pairs={{0,7},{1,2},{2,1},{3,4},{4,3},{5,6},{6,5},{7,0},{8,15},{9,10},{10,... | collective-permute-start | bytes 12296 | tf_op jit(solution)/shard_map/ppermute | solution.py:394
  7.2 0.5 %collective-permute-start.1 = (f32[8,128]{1,0:T(8,128)S(1)}, f32[8,128]{1,0:T(8,128)S(1)}, u32[]{:S(2)}, u32[]{:S(2)}) collective-permute-start(f32[8,128]{1,0:T(8,128)S(1)} %get-tuple-element.27), channel_id=1, source_target_pairs={{0,8},{1,25},{2,10},{3,27},{4,28},{5,13},{6,7},{7,6},{8,0},{9,17},... | collective-permute-start | bytes 12296 | tf_op jit(solution)/shard_map/ppermute | solution.py:394
  7.8 0.0 collective-permute-start
  7.8 1.8 %prepared_elements.1 = (s32[4,8,512]{2,1,0:T(8,128)S(1)}, f32[12,8,512]{2,1,0:T(8,128)S(1)}, f32[9,8,512]{2,1,0:T(8,128)S(1)}, f32[8,512]{1,0:T(8,128)S(1)}, bf1...) custom-call(f32[8,256]{1,0:T(8,128)S(1)} %get-tuple-element.22.table, s32[1,128]{1,0:T(1,128)S(1)} %get-tuple-element.23.sends, ...), custom_call_target="tpu_custom_call" | custom-call | flops 1000000 | bytes 4000000 | tf_op jit(solution)/shard_map/prepared_elements/pallas_call | solution.py:455
  9.5 0.0 collective-permute-done.3.came0
  9.6 0.7 %collective-permute-done.2.came1 = f32[8,128]{1,0:T(8,128)S(1)} collective-permute-done((f32[8,128]{1,0:T(8,128)S(1)}, f32[8,128]{1,0:T(8,128)S(1)}, u32[]{:S(2)}, u32[]{:S(2)}) %collective-permute-start.2) | collective-permute-done | bytes 4128 | tf_op jit(solution)/shard_map/ppermute | solution.py:394
  10.3 0.6 %collective-permute-done.1.came2 = f32[8,128]{1,0:T(8,128)S(1)} collective-permute-done((f32[8,128]{1,0:T(8,128)S(1)}, f32[8,128]{1,0:T(8,128)S(1)}, u32[]{:S(2)}, u32[]{:S(2)}) %collective-permute-start.1) | collective-permute-done | bytes 4128 | tf_op jit(solution)/shard_map/ppermute | solution.py:394
  10.8 0.0 collective-permute-done.came3
  10.8 0.3 jacobian_dets.1
  11.1 9.5 %all_to_all.10 = f32[32,1,128]{2,1,0:T(1,128)S(1)} all-to-all(f32[32,1,128]{2,1,0:T(1,128)S(1)} %bitcast.9), channel_id=1, replica_groups=mesh['dom'=4,'sub'=8] {'dom','sub'}, dimensions={0} | all-to-all | bytes 32768 | tf_op jit(solution)/shard_map/all_to_all | solution.py:489
  20.7 0.8 %element_gradients.1 = (f32[24,256]{1,0:T(8,128)S(1)}, f32[32,4,128]{2,1,0:T(4,128)S(1)}, f32[1,128]{1,0:T(1,128)S(1)}) custom-call(f32[32,128]{1,0:T(8,128)S(1)} %bitcast.8, f32[9,8,512]{2,1,0:T(8,128)S(1)} %get-tuple-element.31.jac_in, f32[8,512]{1,0:T(8,128)S(1)} %get-tuple-element.32.weight, bf16[2,2048,384]{2,1,0:T(8,128)(2,1)S(1)} %get-tuple-element.33.spots, ...), custom_call_target="tpu_custom_call" | custom-call | tf_op jit(solution)/shard_map/element_gradients/pallas_call | solution.py:490
  21.4 9.1 %all_to_all.11.back = f32[32,4,128]{2,1,0:T(4,128)S(1)} all-to-all(f32[32,4,128]{2,1,0:T(4,128)S(1)} %get-tuple-element.34), channel_id=1, replica_groups=mesh['dom'=4,'sub'=8] {'dom','sub'}, dimensions={0} | all-to-all | bytes 131072 | tf_op jit(solution)/shard_map/all_to_all | solution.py:500
  30.5 0.8 %owner_sums.1 = (f32[3,4,256]{2,1,0:T(4,128)}, f32[1,4]{1,0:T(1,128)}, f32[1,4]{1,0:T(1,128)}) custom-call(f32[32,4,128]{2,1,0:T(4,128)S(1)} %all_to_all.11.back, f32[24,256]{1,0:T(8,128)S(1)} %get-tuple-element.35.own, bf16[128,256]{1,0:T(8,128)(2,1)S(1)} %get-tuple-element.36.send_marks, f32[1,128]{1,0:T(1,128)S(1)} %get-tuple-element.37.low), custom_call_target="tpu_custom_call" | custom-call | tf_op jit(solution)/shard_map/owner_sums/pallas_call | solution.py:501
Async XLA Ops:
  1.5 8.1 %collective-permute-start.3 = (f32[8,128]{1,0:T(8,128)S(1)}, f32[8,128]{1,0:T(8,128)S(1)}, u32[]{:S(2)}, u32[]{:S(2)}) collective-permute-start(f32[8,128]{1,0:T(8,128)S(1)} %get-tuple-element.27), channel_id=1, source_target_pairs={{0,24},{1,9},{2,3},{3,2},{4,12},{5,29},{6,30},{7,15},{8,16},{9,1},... | collective-permute-start | bytes 12296 | tf_op jit(solution)/shard_map/ppermute | solution.py:394
  5.4 4.8 %collective-permute-start.2 = (f32[8,128]{1,0:T(8,128)S(1)}, f32[8,128]{1,0:T(8,128)S(1)}, u32[]{:S(2)}, u32[]{:S(2)}) collective-permute-start(f32[8,128]{1,0:T(8,128)S(1)} %get-tuple-element.27), channel_id=1, source_target_pairs={{0,7},{1,2},{2,1},{3,4},{4,3},{5,6},{6,5},{7,0},{8,15},{9,10},{10,... | collective-permute-start | bytes 12296 | tf_op jit(solution)/shard_map/ppermute | solution.py:394
  7.2 3.6 %collective-permute-start.1 = (f32[8,128]{1,0:T(8,128)S(1)}, f32[8,128]{1,0:T(8,128)S(1)}, u32[]{:S(2)}, u32[]{:S(2)}) collective-permute-start(f32[8,128]{1,0:T(8,128)S(1)} %get-tuple-element.27), channel_id=1, source_target_pairs={{0,8},{1,25},{2,10},{3,27},{4,28},{5,13},{6,7},{7,6},{8,0},{9,17},... | collective-permute-start | bytes 12296 | tf_op jit(solution)/shard_map/ppermute | solution.py:394
  7.8 3.1 %collective-permute-start = (f32[8,128]{1,0:T(8,128)S(1)}, f32[8,128]{1,0:T(8,128)S(1)}, u32[]{:S(2)}, u32[]{:S(2)}) collective-permute-start(f32[8,128]{1,0:T(8,128)S(1)} %get-tuple-element.27), channel_id=1, source_target_pairs={{0,1},{1,0},{2,26},{3,11},{4,5},{5,4},{6,14},{7,31},{8,9},{9,8},{1... | collective-permute-start | bytes 12296 | tf_op jit(solution)/shard_map/ppermute | solution.py:394

commit v7 on v6

--- a/solution.py
+++ b/solution.py
@@ -53,11 +53,10 @@
 
 
 def split_three(value):
-    high = value.astype(jnp.bfloat16)
-    rest = value - high.astype(jnp.float32)
-    mid = rest.astype(jnp.bfloat16)
-    low = (rest - mid.astype(jnp.float32)).astype(jnp.bfloat16)
-    return [high, mid, low]
+    high = value.astype(jnp.bfloat16).astype(jnp.float32)
+    rest = value - high
+    mid = rest.astype(jnp.bfloat16).astype(jnp.float32)
+    return jnp.concatenate([high, mid, rest - mid], axis=0).astype(jnp.bfloat16)
 
 
 def marks(row, count):
@@ -289,7 +288,7 @@
             ]
             terms.append([-(edges[0] + edges[1] + edges[2]), *edges])
         values = jnp.concatenate([jnp.concatenate(parts, axis=1) for parts in terms], axis=0)
-        left = jnp.concatenate(split_three(values), axis=0)
+        left = split_three(values)
         height = 4 * LANES
         for half in range(2):
             right = spots[half, block * height : (block + 1) * height, :]
@@ -350,7 +349,7 @@
             moved = pltpu.roll(came[k], turned, 1) if turned else came[k]
             whole = moved if whole is None else jnp.where(wide == k, moved, whole)
         rows.append(whole)
-    left = jnp.concatenate(split_three(jnp.concatenate(rows, axis=0)), axis=0)
+    left = split_three(jnp.concatenate(rows, axis=0))
     found = jnp.dot(left, send_marks[...], preferred_element_type=jnp.float32)
     height = 3 * SUBS
     found = found[:height] + found[height : 2 * height] + found[2 * height :]

time: 31.6 us -> 31.6 us (level)
  no operation moved by 1% of the time
where the time goes in v7:
time: 31.6 us; the launch traced here: 31.3 us
  blocking collectives  18.6 us (59%)
  starting transfers between devices  6.3 us (20%)
  Pallas kernels  4.48 us (14%)
  waiting for transfers between devices  1.29 us (4%)
  between operations  0.66 us (2%)
    all_to_all x1, blocking collectives, per_device(): lax.all_to_all(lows.reshape(count, 1, LANES), AXES, 0, 0)  9.51 us
    all_to_all x1, blocking collectives, per_device(): back = lax.all_to_all(back, AXES, 0, 0)  9.08 us
    ppermute x4, starting transfers between devices, exchanged(): lax.ppermute(tile, AXES, [(dom * subs + sub, partner(orders[sub][step], d...  6.3 us
    pallas_call x1, Pallas kernels, per_device(): pl.pallas_call(functools.partial(prepare_kernel, blocks), in_specs=[pl.Bl...  1.76 us
    ppermute x4, waiting for transfers between devices, exchanged(): lax.ppermute(tile, AXES, [(dom * subs + sub, partner(orders[sub][step], d...  1.29 us
    pallas_call x1, Pallas kernels, per_device(): pl.pallas_call(send_kernel, in_specs=[hbm] * 5, out_shape=(shaped((SUBS,...  0.83 us
    pallas_call x1, Pallas kernels, per_device(): pl.pallas_call(functools.partial(final_kernel, subs, doms, float(elems *...  0.82 us
    pallas_call x1, Pallas kernels, per_device(): pl.pallas_call(functools.partial(grad_kernel, blocks, subs, doms), out_sh...  0.77 us
  transfers between devices with their start and end apart: 4, of which 2 were waited for; matrix products, arithmetic and copies ran while one was open for 0% of the time, Pallas kernels for 6%

profile of v7, /device:TPU:0, one launch (start us, length us, event | category | flops | bytes accessed | tf_op | source)
XLA Modules:
  0.0 31.3 jit_solution(3128337214781082796)
XLA Ops:
  0.6 0.8 %outgoing_nodes.1 = (f32[8,128]{1,0:T(8,128)S(1)}, f32[8,256]{1,0:T(8,128)S(1)}, s32[1,128]{1,0:T(1,128)S(1)}, s32[1,128]{1,0:T(1,128)S(1)}, s32[4,1024]{1,0:T(4,128)S(1)}) custom-call(f32[3,256]{1,0:T(4,128)} %coords.1, f32[3,256]{1,0:T(4,128)} %direction.1, s32[1,128]{1,0:T(1,128)} %send.1, s32[1,128]{1,0:T(1,128)} %slots.1, s32[4,1024]{1,0:T(4,128)} %connect.1), custom_call_target="tpu_custom_call" | custom-call | tf_op jit(solution)/shard_map/outgoing_nodes/pallas_call | solution.py:436
  1.5 4.0 %collective-permute-start.3 = (f32[8,128]{1,0:T(8,128)S(1)}, f32[8,128]{1,0:T(8,128)S(1)}, u32[]{:S(2)}, u32[]{:S(2)}) collective-permute-start(f32[8,128]{1,0:T(8,128)S(1)} %get-tuple-element.27), channel_id=1, source_target_pairs={{0,24},{1,9},{2,3},{3,2},{4,12},{5,29},{6,30},{7,15},{8,16},{9,1},... | collective-permute-start | bytes 12296 | tf_op jit(solution)/shard_map/ppermute | solution.py:393
  5.4 1.8 %collective-permute-start.2 = (f32[8,128]{1,0:T(8,128)S(1)}, f32[8,128]{1,0:T(8,128)S(1)}, u32[]{:S(2)}, u32[]{:S(2)}) collective-permute-start(f32[8,128]{1,0:T(8,128)S(1)} %get-tuple-element.27), channel_id=1, source_target_pairs={{0,7},{1,2},{2,1},{3,4},{4,3},{5,6},{6,5},{7,0},{8,15},{9,10},{10,... | collective-permute-start | bytes 12296 | tf_op jit(solution)/shard_map/ppermute | solution.py:393
  7.2 0.5 %collective-permute-start.1 = (f32[8,128]{1,0:T(8,128)S(1)}, f32[8,128]{1,0:T(8,128)S(1)}, u32[]{:S(2)}, u32[]{:S(2)}) collective-permute-start(f32[8,128]{1,0:T(8,128)S(1)} %get-tuple-element.27), channel_id=1, source_target_pairs={{0,8},{1,25},{2,10},{3,27},{4,28},{5,13},{6,7},{7,6},{8,0},{9,17},... | collective-permute-start | bytes 12296 | tf_op jit(solution)/shard_map/ppermute | solution.py:393
  7.8 0.0 collective-permute-start
  7.8 1.8 %prepared_elements.1 = (s32[4,8,512]{2,1,0:T(8,128)S(1)}, f32[12,8,512]{2,1,0:T(8,128)S(1)}, f32[9,8,512]{2,1,0:T(8,128)S(1)}, f32[8,512]{1,0:T(8,128)S(1)}, bf1...) custom-call(f32[8,256]{1,0:T(8,128)S(1)} %get-tuple-element.22.table, s32[1,128]{1,0:T(1,128)S(1)} %get-tuple-element.23.sends, ...), custom_call_target="tpu_custom_call" | custom-call | flops 1000000 | bytes 4000000 | tf_op jit(solution)/shard_map/prepared_elements/pallas_call | solution.py:454
  9.5 0.0 collective-permute-done.3.came0
  9.6 0.7 %collective-permute-done.2.came1 = f32[8,128]{1,0:T(8,128)S(1)} collective-permute-done((f32[8,128]{1,0:T(8,128)S(1)}, f32[8,128]{1,0:T(8,128)S(1)}, u32[]{:S(2)}, u32[]{:S(2)}) %collective-permute-start.2) | collective-permute-done | bytes 4128 | tf_op jit(solution)/shard_map/ppermute | solution.py:393
  10.3 0.6 %collective-permute-done.1.came2 = f32[8,128]{1,0:T(8,128)S(1)} collective-permute-done((f32[8,128]{1,0:T(8,128)S(1)}, f32[8,128]{1,0:T(8,128)S(1)}, u32[]{:S(2)}, u32[]{:S(2)}) %collective-permute-start.1) | collective-permute-done | bytes 4128 | tf_op jit(solution)/shard_map/ppermute | solution.py:393
  10.8 0.0 collective-permute-done.came3
  10.8 0.3 jacobian_dets.1
  11.1 9.5 %all_to_all.10 = f32[32,1,128]{2,1,0:T(1,128)S(1)} all-to-all(f32[32,1,128]{2,1,0:T(1,128)S(1)} %bitcast.9), channel_id=1, replica_groups=mesh['dom'=4,'sub'=8] {'dom','sub'}, dimensions={0} | all-to-all | bytes 32768 | tf_op jit(solution)/shard_map/all_to_all | solution.py:488
  20.7 0.8 %element_gradients.1 = (f32[24,256]{1,0:T(8,128)S(1)}, f32[32,4,128]{2,1,0:T(4,128)S(1)}, f32[1,128]{1,0:T(1,128)S(1)}) custom-call(f32[32,128]{1,0:T(8,128)S(1)} %bitcast.8, f32[9,8,512]{2,1,0:T(8,128)S(1)} %get-tuple-element.31.jac_in, f32[8,512]{1,0:T(8,128)S(1)} %get-tuple-element.32.weight, bf16[2,2048,384]{2,1,0:T(8,128)(2,1)S(1)} %get-tuple-element.33.spots, ...), custom_call_target="tpu_custom_call" | custom-call | tf_op jit(solution)/shard_map/element_gradients/pallas_call | solution.py:489
  21.4 9.1 %all_to_all.11.back = f32[32,4,128]{2,1,0:T(4,128)S(1)} all-to-all(f32[32,4,128]{2,1,0:T(4,128)S(1)} %get-tuple-element.34), channel_id=1, replica_groups=mesh['dom'=4,'sub'=8] {'dom','sub'}, dimensions={0} | all-to-all | bytes 131072 | tf_op jit(solution)/shard_map/all_to_all | solution.py:499
  30.5 0.8 %owner_sums.1 = (f32[3,4,256]{2,1,0:T(4,128)}, f32[1,4]{1,0:T(1,128)}, f32[1,4]{1,0:T(1,128)}) custom-call(f32[32,4,128]{2,1,0:T(4,128)S(1)} %all_to_all.11.back, f32[24,256]{1,0:T(8,128)S(1)} %get-tuple-element.35.own, bf16[128,256]{1,0:T(8,128)(2,1)S(1)} %get-tuple-element.36.send_marks, f32[1,128]{1,0:T(1,128)S(1)} %get-tuple-element.37.low), custom_call_target="tpu_custom_call" | custom-call | tf_op jit(solution)/shard_map/owner_sums/pallas_call | solution.py:500
Async XLA Ops:
  1.5 8.1 %collective-permute-start.3 = (f32[8,128]{1,0:T(8,128)S(1)}, f32[8,128]{1,0:T(8,128)S(1)}, u32[]{:S(2)}, u32[]{:S(2)}) collective-permute-start(f32[8,128]{1,0:T(8,128)S(1)} %get-tuple-element.27), channel_id=1, source_target_pairs={{0,24},{1,9},{2,3},{3,2},{4,12},{5,29},{6,30},{7,15},{8,16},{9,1},... | collective-permute-start | bytes 12296 | tf_op jit(solution)/shard_map/ppermute | solution.py:393
  5.4 4.8 %collective-permute-start.2 = (f32[8,128]{1,0:T(8,128)S(1)}, f32[8,128]{1,0:T(8,128)S(1)}, u32[]{:S(2)}, u32[]{:S(2)}) collective-permute-start(f32[8,128]{1,0:T(8,128)S(1)} %get-tuple-element.27), channel_id=1, source_target_pairs={{0,7},{1,2},{2,1},{3,4},{4,3},{5,6},{6,5},{7,0},{8,15},{9,10},{10,... | collective-permute-start | bytes 12296 | tf_op jit(solution)/shard_map/ppermute | solution.py:393
  7.2 3.6 %collective-permute-start.1 = (f32[8,128]{1,0:T(8,128)S(1)}, f32[8,128]{1,0:T(8,128)S(1)}, u32[]{:S(2)}, u32[]{:S(2)}) collective-permute-start(f32[8,128]{1,0:T(8,128)S(1)} %get-tuple-element.27), channel_id=1, source_target_pairs={{0,8},{1,25},{2,10},{3,27},{4,28},{5,13},{6,7},{7,6},{8,0},{9,17},... | collective-permute-start | bytes 12296 | tf_op jit(solution)/shard_map/ppermute | solution.py:393
  7.8 3.1 %collective-permute-start = (f32[8,128]{1,0:T(8,128)S(1)}, f32[8,128]{1,0:T(8,128)S(1)}, u32[]{:S(2)}, u32[]{:S(2)}) collective-permute-start(f32[8,128]{1,0:T(8,128)S(1)} %get-tuple-element.27), channel_id=1, source_target_pairs={{0,1},{1,0},{2,26},{3,11},{4,5},{5,4},{6,14},{7,31},{8,9},{9,8},{1... | collective-permute-start | bytes 12296 | tf_op jit(solution)/shard_map/ppermute | solution.py:393
